TPU v7x, 32 devices: a whole 2x2x4 slice. The times are simulated.
32 devices in a mesh: band: 8 (over y, x, core), col: 4 (over z).
Axes of the slice: x: 2, y: 2, z: 4, core: 2. Of those that a mesh axis runs over, the one named last changes fastest.
Arguments:
- valence: bfloat16 [8, 128, 128, 128], P('band', 'col'), may hold values from -6 to 6
- conduction: bfloat16 [24, 128, 128, 128], P('band', 'col'), may hold values from -6 to 6
- energy_val: float32 [8], replicated, may hold values from -12 to -2
- energy_cond: float32 [24], P('band'), may hold values from 1 to 20
- kept: int32 [3, 1536], replicated, may hold values from 0 to 127
- plan: int32 [3], replicated, may hold values from 0 to 7
Outputs:
- response: float32 [1536, 1536], P('band', 'col')
All inputs are finite; a program needn't handle non-finite values.
Results may differ from a plain program's by a relative error of at most 0.012.
Values may be sent and summed in bfloat16 or wider, within the bound.
No kernel may reach another device: no remote copies, remote signals or barrier semaphores. Data moves between devices by JAX's collectives and lax.ppermute only.
A program may use at most 192 MiB of HBM per device.

v0:
```python
import jax
import jax.numpy as jnp
from jax import lax
from jax.sharding import PartitionSpec as P


def broadcast(value, axis, root):
    mine = lax.axis_index(axis) == root
    return lax.psum(jnp.where(mine, value, jnp.zeros_like(value)), axis)


def cas_table(frequency, position, length):
    phase_index = frequency[:, None] * position[None, :] % length
    angle_value = 2.0 * jnp.pi / length * phase_index.astype(jnp.float32)
    return jnp.cos(angle_value) + jnp.sin(angle_value)


def per_device(valence, conduction, energy_val, energy_cond, kept, plan):
    band_local = conduction.shape[0]
    x_local = conduction.shape[1]
    length = conduction.shape[2]
    width_keep = kept.shape[1]
    held_count = valence.shape[0]
    n_band = lax.axis_size("band")
    n_col = lax.axis_size("col")
    position = jnp.arange(length, dtype=jnp.int32)
    x_global = lax.axis_index("col") * x_local + jnp.arange(x_local, dtype=jnp.int32)
    table_z = cas_table(position, position, length).astype(jnp.bfloat16)
    table_x = cas_table(kept[0], x_global, length).T
    flat_index = kept[1] * length + kept[2]
    norm_factor = length ** (-1.5)
    partial_list = []
    weight_list = []
    for round_index in range(plan.shape[0]):
        target = plan[round_index]
        root_index = target // held_count
        own_band = lax.dynamic_index_in_dim(valence, target % held_count, 0, keepdims=False)
        valence_band = broadcast(own_band, "band", root_index)
        product = (valence_band.astype(jnp.float32)[None] * conduction.astype(jnp.float32)).astype(
            jnp.bfloat16
        )
        sectioned = jnp.dot(
            product.reshape(-1, length), table_z, preferred_element_type=jnp.float32
        )
        sectioned = sectioned.astype(jnp.bfloat16).reshape(band_local, x_local, length, length)
        along_y = jnp.einsum(
            "pxyk,yj->pxjk", sectioned, table_z, preferred_element_type=jnp.float32
        )
        picked = jnp.take(along_y.reshape(band_local, x_local, length * length), flat_index, axis=2)
        partial_list.append(jnp.sum(picked * table_x[None], axis=1) * norm_factor)
        weight_list.append(1.0 / (energy_cond - energy_val[target]))
    partial_all = jnp.concatenate(partial_list, axis=0)
    weights = jnp.concatenate(weight_list, axis=0)
    coeffs = lax.psum(partial_all, "col")
    plain_coeffs = coeffs.astype(jnp.bfloat16)
    weighted = (weights[:, None] * coeffs).astype(jnp.bfloat16)
    col_width = width_keep // n_col
    col_piece = lax.dynamic_slice_in_dim(
        plain_coeffs, lax.axis_index("col") * col_width, col_width, 1
    )
    row_piece = lax.all_to_all(weighted, "band", split_axis=1, concat_axis=0, tiled=True)
    response_tile = lax.dot_general(
        row_piece,
        lax.all_gather(col_piece, "band", axis=0, tiled=True),
        (((0,), (0,)), ((), ())),
        preferred_element_type=jnp.float32,
    )
    factor = (plan.shape[0] * band_local * n_band) ** (-0.5)
    return -response_tile * factor


def solution(mesh):
    return jax.shard_map(
        per_device,
        mesh=mesh,
        in_specs=(
            P("band", "col", None, None),
            P("band", "col", None, None),
            P(),
            P("band"),
            P(),
            P(),
        ),
        out_specs=P("band", "col"),
        check_vma=False,
    )
```

profile of v0, /device:TPU:0, one launch (start us, length us, event | category | flops | bytes accessed | tf_op | source)
XLA Modules:
  0.0 269.1 jit_solution(10730516050311891011)
XLA Ops:
  6.5 0.0 all-reduce.3.cloned.1.call-start
  6.5 1.4 fusion.45
  9.8 0.0 copy-start.4
  9.8 3.0 %select_bitcast_fusion = (bf16[32,128,128]{2,1,0:T(8,128)(2,1)}, bf16[32,128,128]{2,1,0:T(8,128)(2,1)}, bf16[32,128,128]{2,1,0:T(8,128)(2,1)}) fusion(bf16[1,32,128,128]{3,2,1,0:T(8,128)(2,1)} %param.8, pred[]{:T(512)S(6)} %eq.19, pred[]{:T(512)S(6)} %eq.17, pred[]{:T(512)S(6)} %eq.18), kind=kLoop, calls=%fused_computation.23 | loop fusion | flops 1572864 | bytes 4194307 | tf_op jit(solution)/shard_map/jit(_where)/select_n | solution.py:9
  12.8 0.0 all-reduce.3.cloned.1.call-update
  16.7 0.0 copy-done.4
  16.8 0.9 sine_add_fusion
  17.6 1.2 copy.33
  20.7 0.0 copy-done.5
  20.7 0.7 fusion.44
  21.4 0.0 copy-done.6
  21.4 1.9 subtract_divide_fusion.2
  23.3 0.1 pad_maximum_fusion.1
  23.4 62.2 %all-reduce.3.cloned.1.call-done = (bf16[32,128,128]{2,1,0:T(8,128)(2,1)}, bf16[32,128,128]{2,1,0:T(8,128)(2,1)}, bf16[32,128,128]{2,1,0:T(8,128)(2,1)}) async-done(((bf16[32,128,128]{2,1,0:T(8,128)(2,1)}, bf16[32,128,128]{2,1,0:T(8,128)(2,1)}, bf16[32,128,128]{2,1,0:T(8,128)(2,1)}), (bf16[32,128,128]{2,1,0:T(8,128)(2,1)}, bf16[32,128,128]{2,1,0:T(8,128)(2,1)}, ...) | async-done | bytes 3145744 | tf_op jit(solution)/shard_map/psum | solution.py:9
  85.6 1.6 convert_element_type.74
  87.2 0.0 copy-done.3
  87.2 0.0 copy-start.1
  87.2 0.2 convert_element_type.79
  87.5 0.0 copy-done.2
  87.5 0.2 convert_element_type.82
  87.7 1.5 copy-done.1
  89.2 3.0 %fusion.2 = (bf16[3,32,128,128]{3,2,1,0:T(8,128)(2,1)S(1)}, bf16[3,32,128,128]{3,2,1,0:T(8,128)(2,1)}, bf16[3,32,128,128]{3,2,1,0:T(8,128)(2,1)S(1)}) fusion(bf16[3,32,128,128]{3,2,1,0:T(8,128)(2,1)S(1)} %copy-done.1, f32[32,128,128]{2,1,0:T(8,128)S(1)} %convert_element_type.82, f32[32,128,128]{2,1,0:T(8,128)S(1)} %convert_element_type.79, ...), kind=kLoop, calls=%fused_computation.11 | loop fusion | flops 11010048 | bytes 18874368 | tf_op jit(solution)/shard_map/convert_element_type | solution.py:39
  92.2 1.2 convolution_convert_fusion.2
  93.4 3.8 %convolution_bitcast_fusion.2 = f32[3,32,128,128]{3,2,1,0:T(8,128)} fusion(bf16[3,32,128,128]{3,2,1,0:T(8,128)(2,1)S(1)} %bitcast.68), kind=kOutput, calls=%fused_computation.20 | convolution fusion | flops 402915328 | bytes 9437184 | tf_op jit(solution)/shard_map/pxyk,yj->pxjk/dot_general | solution.py:46
  97.2 18.9 %copy.41 = f32[3,32,128,128]{1,0,3,2:T(4,128)} copy(f32[3,32,128,128]{3,2,1,0:T(8,128)} %convolution_bitcast_fusion.2) | data formatting | bytes 12582912 | tf_op jit(solution)/shard_map/reshape | solution.py:49
  116.2 3.1 %convolution_convert_fusion.1 = bf16[12288,128]{1,0:T(8,128)(2,1)S(1)} fusion(bf16[12288,128]{1,0:T(8,128)(2,1)} %bitcast.72), kind=kOutput, calls=%fused_computation.4 | convolution fusion | flops 404488192 | bytes 6291456 | tf_op jit(solution)/shard_map/dot_general | solution.py:42
  119.3 3.9 %convolution_bitcast_fusion.1 = f32[3,32,128,128]{3,2,1,0:T(8,128)} fusion(bf16[3,32,128,128]{3,2,1,0:T(8,128)(2,1)S(1)} %bitcast.69), kind=kOutput, calls=%fused_computation.19 | convolution fusion | flops 402915328 | bytes 9437184 | tf_op jit(solution)/shard_map/pxyk,yj->pxjk/dot_general | solution.py:46
  123.2 18.9 %copy.42 = f32[3,32,128,128]{1,0,3,2:T(4,128)} copy(f32[3,32,128,128]{3,2,1,0:T(8,128)} %convolution_bitcast_fusion.1) | data formatting | bytes 12582912 | tf_op jit(solution)/shard_map/reshape | solution.py:49
  142.1 9.3 %gather_fusion = f32[1536,3,32]{2,1,0:T(4,128)} fusion(f32[3,32,16384]{1,0,2:T(4,128)} %bitcast.65, s32[2048]{0:T(1024)S(1)} %pad_clamp_fusion), kind=kCustom, calls=%fused_computation.clone | custom fusion | bytes 1185792 | tf_op jit(solution)/shard_map/jit(_take)/gather | solution.py:49
  151.4 9.3 %gather_fusion.1 = f32[1536,3,32]{2,1,0:T(4,128)} fusion(f32[3,32,16384]{1,0,2:T(4,128)} %bitcast.66, s32[2048]{0:T(1024)S(1)} %pad_clamp_fusion), kind=kCustom, calls=%fused_computation.1.clone | custom fusion | bytes 1185792 | tf_op jit(solution)/shard_map/jit(_take)/gather | solution.py:49
  160.7 1.2 convolution_convert_fusion
  162.0 3.8 %convolution_bitcast_fusion = f32[3,32,128,128]{3,2,1,0:T(8,128)} fusion(bf16[3,32,128,128]{3,2,1,0:T(8,128)(2,1)S(1)} %bitcast.70), kind=kOutput, calls=%fused_computation.18 | convolution fusion | flops 402915328 | bytes 9437184 | tf_op jit(solution)/shard_map/pxyk,yj->pxjk/dot_general | solution.py:46
  165.8 19.1 %copy.43 = f32[3,32,128,128]{1,0,3,2:T(4,128)} copy(f32[3,32,128,128]{3,2,1,0:T(8,128)} %convolution_bitcast_fusion) | data formatting | bytes 12582912 | tf_op jit(solution)/shard_map/reshape | solution.py:49
  184.9 9.5 %gather_fusion.2 = f32[1536,3,32]{2,1,0:T(4,128)} fusion(f32[3,32,16384]{1,0,2:T(4,128)} %bitcast.67, s32[2048]{0:T(1024)S(1)} %pad_clamp_fusion), kind=kCustom, calls=%fused_computation.2.clone | custom fusion | bytes 1185792 | tf_op jit(solution)/shard_map/jit(_take)/gather | solution.py:49
  194.3 0.0 copy-done
  194.3 28.2 %fusion.5 = (f32[3,1536]{0,1:T(8,128)}, f32[3,1536]{0,1:T(8,128)}, f32[3,1536]{0,1:T(8,128)}) fusion(f32[1536,3,32]{2,1,0:T(4,128)S(1)} %copy-done, f32[32,1536]{0,1:T(8,128)} %copy.33, pred[1536]{0:T(1024)(128)(4,1)S(1)} %compare_and_fusion, f32[1536,3,32]{2,1,0:T(4,128)} %gather_fusion.1, f32[1536,3,32]{2,1,0:T(4,128)} %gather_fusion.2), kind=kLoop, calls=%fused_computation.17 | loop fusion | flops 1313280 | bytes 2022912 | tf_op jit(solution)/shard_map/reduce_sum | solution.py:50
  222.5 1.4 copy.36
  223.9 1.4 copy.38
  225.3 1.4 copy.34
  226.8 20.3 %psum.31 = f32[9,1536]{1,0:T(8,128)S(1)} all-reduce(f32[9,1536]{1,0:T(8,128)S(1)} %pad_maximum_fusion), channel_id=1, replica_groups=mesh['band'=8,'col'=4] {'col'}, use_global_device_ids=true, to_apply=%region_6.8 | all-reduce | flops 13824 | bytes 110592 | tf_op jit(solution)/shard_map/psum | solution.py:54
  247.1 0.1 multiply_convert_fusion
  247.2 0.1 all_to_all.14
  247.3 0.7 reshape.147
  248.1 3.3 %all-to-all-start = ((bf16[8,2,864]{2,1,0:T(2,128)(2,1)}), bf16[8,2,864]{2,1,0:T(2,128)(2,1)S(1)}, u32[]{:S(2)}, u32[]{:S(2)}) async-start(bf16[8,2,864]{2,1,0:T(2,128)(2,1)} %reshape.147), calls=%async_computation | async-start | bytes 57344 | tf_op jit(solution)/shard_map/all_to_all | solution.py:61
  251.4 9.6 %all-gather = bf16[8,9,384]{2,1,0:T(8,128)(2,1)S(1)} all-gather(bf16[1,9,384]{2,1,0:T(8,128)(2,1)S(1)} %fusion.19), channel_id=1, replica_groups=mesh['band'=8,'col'=4] {'band'}, dimensions={0}, use_global_device_ids=true | all-gather | bytes 62208 | tf_op jit(solution)/shard_map/all_gather | solution.py:64
  261.1 0.0 all-to-all-done
  261.1 0.1 reshape.148
  261.3 0.9 fusion.6
  (18 shorter events, 0.2 us)
Async XLA Ops:
  6.5 79.1 %all-reduce.3.cloned.1.call-start = ((), (), s32[]{:S(2)}) async-start(), calls=%async_computation.1 | async-start | bytes 6291456 | tf_op jit(solution)/shard_map/psum | solution.py:9
  9.8 6.9 %copy-start.4 = (s32[3,1536]{1,0:T(4,128)S(1)}, s32[3,1536]{1,0:T(4,128)}, u32[]{:S(2)}) copy-start(s32[3,1536]{1,0:T(4,128)} %param.12) | copy-start | bytes 55300
  12.8 7.9 %copy-start.5 = (f32[8]{0:T(128)S(1)}, f32[8]{0:T(128)}, u32[]{:S(2)}) copy-start(f32[8]{0:T(128)} %param.10) | copy-start | bytes 100
  12.8 8.6 %copy-start.6 = (f32[3]{0:T(128)S(1)}, f32[3]{0:T(128)}, u32[]{:S(2)}) copy-start(f32[3]{0:T(128)} %param.11) | copy-start | bytes 40
  85.6 1.6 copy-start.3
  85.6 1.9 copy-start.2
  87.2 1.9 copy-start.1
  165.8 28.6 %copy-start = (f32[1536,3,32]{2,1,0:T(4,128)S(1)}, f32[1536,3,32]{2,1,0:T(4,128)}, u32[]{:S(2)}) copy-start(f32[1536,3,32]{2,1,0:T(4,128)} %gather_fusion) | copy-start | bytes 1769476
  248.1 13.0 %all-to-all-start = ((bf16[8,2,864]{2,1,0:T(2,128)(2,1)}), bf16[8,2,864]{2,1,0:T(2,128)(2,1)S(1)}, u32[]{:S(2)}, u32[]{:S(2)}) async-start(bf16[8,2,864]{2,1,0:T(2,128)(2,1)} %reshape.147), calls=%async_computation | async-start | bytes 57344 | tf_op jit(solution)/shard_map/all_to_all | solution.py:61
Sparse Core Ops, SparseCore 0:
  13.0 72.5 all-reduce.2
where the time goes:
time: 272 us; the launch traced here: 269 us
  local copies, waits for them, and re-layouts  95 us (35%)
  waiting for transfers between devices  62.2 us (23%)
  other arithmetic  39.3 us (14%)
  blocking collectives  29.9 us (11%)
  between operations  21.3 us (8%)
  matrix products  18 us (7%)
  starting transfers between devices  3.34 us (1%)
    psum x1, waiting for transfers between devices, broadcast(): return lax.psum(jnp.where(mine, value, jnp.zeros_like(value)), axis)  62.2 us
    reshape x3, local copies, waits for them, and re-layouts, per_device(): along_y.reshape(band_local, x_local, length * length)  57 us
    reduce_sum x1, other arithmetic, per_device(): partial_list.append(jnp.sum(picked * table_x[None], axis=1) * norm_factor)  28.2 us
    gather x3, local copies, waits for them, and re-layouts, per_device(): jnp.take(along_y.reshape(band_local, x_local, length * length), flat_inde...  28.1 us
    psum x1, blocking collectives, per_device(): coeffs = lax.psum(partial_all, 'col')  20.3 us
    dot_general x3, matrix products, per_device(): jnp.einsum('pxyk,yj->pxjk', sectioned, table_z, preferred_element_type=jn...  11.5 us
    all_gather x1, blocking collectives, per_device(): lax.all_gather(col_piece, 'band', axis=0, tiled=True)  9.63 us
    dot_general x3, matrix products, per_device(): jnp.dot(product.reshape(-1, length), table_z, preferred_element_type=jnp....  5.56 us
  transfers between devices with their start and end apart: 2, of which 1 were waited for; matrix products, arithmetic and copies ran while one was open for 2% of the time, Pallas kernels for 0%

commit v1 on v0

v1 whole, which is shorter than its diff:
```python
import jax
import jax.numpy as jnp
from jax import lax
from jax.experimental import pallas as pl
from jax.experimental.pallas import tpu as pltpu
from jax.sharding import PartitionSpec as P

LANES = 128
NT = (((1,), (1,)), ((), ()))


def cas_of(phase, length):
    angle_value = 2.0 * jnp.pi / length * phase.astype(jnp.float32)
    return jnp.cos(angle_value) + jnp.sin(angle_value)


def round_kernel(index_ref, va_ref, vb_ref, c0_ref, c1_ref, table_ref, tx_ref, out_ref, s_ref, a_ref, g_ref):
    half, length = va_ref.shape[0], va_ref.shape[1]
    bands = c0_ref.shape[0]
    planes = 2 * half
    lanes = tx_ref.shape[1]
    keep = tx_ref.shape[0]
    table = table_ref[...]

    def transform_z(c_ref, band_base):
        def step(i, carry):
            band, x = i // half, (i % half) * 2
            in_a = x < half
            xa = jnp.minimum(x, half - 2)
            xb = jnp.maximum(x - half, 0)
            v = jnp.where(in_a, va_ref[pl.ds(xa, 2)], vb_ref[pl.ds(xb, 2)])
            product = (v * c_ref[band, pl.ds(x, 2)]).reshape(2 * length, length)
            out = lax.dot_general(table, product, NT, preferred_element_type=jnp.float32)
            out = out.astype(jnp.bfloat16).astype(jnp.float32)
            row = (band_base + band) * planes + x
            s_ref[pl.ds(row, length, stride=lanes), :] = out[:, :length]
            s_ref[pl.ds(row + 1, length, stride=lanes), :] = out[:, length:]
            return carry

        lax.fori_loop(0, bands * half, step, 0, unroll=4)

    transform_z(c0_ref, 0)
    transform_z(c1_ref, bands)

    def transform_y(j, carry):
        rows = s_ref[pl.ds(pl.multiple_of(j * 2 * lanes, 2 * lanes), 2 * lanes), :].astype(jnp.bfloat16)
        out = lax.dot_general(table, rows, NT, preferred_element_type=jnp.float32)
        base = pl.multiple_of(j * 2 * length, 2 * length)
        a_ref[pl.ds(base, length), :] = out[:, :lanes]
        a_ref[pl.ds(base + length, length), :] = out[:, lanes:]
        return carry

    lax.fori_loop(0, length // 2, transform_y, 0, unroll=4)

    def pick(q, carry):
        g_ref[pl.ds(q, 1), :] = a_ref[pl.ds(index_ref[q], 1), :]
        return carry

    lax.fori_loop(0, keep, pick, 0, unroll=16)

    used = 2 * bands * planes
    lane = lax.broadcasted_iota(jnp.int32, (keep, lanes), 1)
    scaled = jnp.where(lane < used, g_ref[...] * tx_ref[...], 0.0)
    high = scaled.astype(jnp.bfloat16)
    low = (scaled - high.astype(jnp.float32)).astype(jnp.bfloat16)
    rows = out_ref.shape[0]
    owner = lax.broadcasted_iota(jnp.int32, (rows, lanes), 1) // planes
    select = (owner == lax.broadcasted_iota(jnp.int32, (rows, lanes), 0)).astype(jnp.bfloat16)
    out_ref[...] = lax.dot_general(select, high, NT, preferred_element_type=jnp.float32) + lax.dot_general(
        select, low, NT, preferred_element_type=jnp.float32
    )


def round_coeffs(index, va, vb, c0, c1, table, tx):
    keep, lanes = tx.shape
    length = table.shape[0]
    rows = -(-2 * c0.shape[0] // 8) * 8
    vmem = pl.BlockSpec(memory_space=pltpu.VMEM)
    return pl.pallas_call(
        round_kernel,
        out_shape=jax.ShapeDtypeStruct((rows, keep), jnp.float32),
        in_specs=[pl.BlockSpec(memory_space=pltpu.SMEM)] + [vmem] * 6,
        out_specs=vmem,
        scratch_shapes=[
            pltpu.VMEM((length * lanes, length), jnp.float32),
            pltpu.VMEM((length * length, lanes), jnp.float32),
            pltpu.VMEM((keep, lanes), jnp.float32),
        ],
        compiler_params=pltpu.CompilerParams(vmem_limit_bytes=30 * 2**20),
        cost_estimate=pl.CostEstimate(flops=4 * 10**9, bytes_accessed=12 * 2**20, transcendentals=0),
        name="round_coeffs",
    )(index, va, vb, c0, c1, table, tx)


def per_device(valence, conduction, energy_val, energy_cond, kept, plan):
    band_local, x_local, length = conduction.shape[:3]
    keep = kept.shape[1]
    held = valence.shape[0]
    rounds = plan.shape[0]
    n_band = lax.axis_size("band")
    n_col = lax.axis_size("col")
    n_pair = n_band // 2
    bits = n_pair.bit_length() - 1
    me = lax.axis_index("band")
    side, group = me % 2, me // 2
    col = lax.axis_index("col")
    x_half = x_local // 2

    def swap(value, mask):
        return lax.ppermute(value, "band", [(i, i ^ mask) for i in range(n_band)])

    def halves(value):
        low, high = value[:, :x_half], value[:, x_half:]
        return jnp.where(side == 0, low, high), jnp.where(side == 0, high, low)

    v_mine, v_other = halves(valence)
    v_swapped = swap(v_other, 1)
    c_mine, c_other = halves(conduction)
    c_swapped = swap(c_other, 1)
    c0 = jnp.where(side == 0, c_mine, c_swapped)
    c1 = jnp.where(side == 0, c_swapped, c_mine)

    root = plan // held
    local = plan % held
    relative = (root // 2) ^ group
    root_side = root % 2

    def slot(values, r):
        return lax.dynamic_index_in_dim(values, local[r], 0, keepdims=False)

    def spread(mine, swapped, order):
        if 2 * held <= rounds and order:
            bit = order[0]
            far_mine, far_swapped = swap(jnp.concatenate([mine, swapped]), 2 << bit).reshape(2, *mine.shape)
            slots = []
            for r in range(rounds):
                same = root_side[r] == side
                near = jnp.where(same, slot(mine, r), slot(swapped, r))
                far = jnp.where(same, slot(far_mine, r), slot(far_swapped, r))
                slots.append(jnp.where((relative[r] >> bit) & 1 == 0, near, far))
            order = order[1:]
        else:
            slots = [jnp.where(root_side[r] == side, slot(mine, r), slot(swapped, r)) for r in range(rounds)]
        for bit in order:
            far = [swap(s, 2 << bit) for s in slots]
            slots = [jnp.where((relative[r] >> bit) & 1 == 0, slots[r], far[r]) for r in range(rounds)]
        return slots

    cut = x_half // 2
    part_a = spread(v_mine[:, :cut], v_swapped[:, :cut], list(range(bits)))
    part_b = spread(v_mine[:, cut:], v_swapped[:, cut:], list(range(bits))[::-1])

    position = jnp.arange(length, dtype=jnp.int32)
    table = cas_of(position[:, None] * position[None, :] % length, length).astype(jnp.bfloat16)
    used = 2 * band_local * x_half
    lanes = -(-used // LANES) * LANES
    x_global = col * x_local + side * x_half + jnp.arange(lanes, dtype=jnp.int32) % x_half
    tx = cas_of(kept[0][:, None] * x_global[None, :] % length, length) * length ** (-1.5)
    index = kept[2] * length + kept[1]

    partial = [round_coeffs(index, part_a[r], part_b[r], c0, c1, table, tx) for r in range(rounds)]

    first = jnp.concatenate([p[:band_local] for p in partial])
    second = jnp.concatenate([p[band_local : 2 * band_local] for p in partial])
    mine = jnp.where(side == 0, first, second)
    coeffs = mine + swap(jnp.where(side == 0, second, first), 1)
    sent = coeffs.astype(jnp.bfloat16)
    for shift in range(1, n_col):
        moved = lax.ppermute(sent, "col", [(i, (i + shift) % n_col) for i in range(n_col)])
        coeffs = coeffs + moved.astype(jnp.float32)
    weights = jnp.concatenate([1.0 / (energy_cond - energy_val[plan[r]]) for r in range(rounds)])
    weighted = (weights[:, None] * coeffs).astype(jnp.bfloat16)
    plain = coeffs.astype(jnp.bfloat16)

    col_width, row_width = keep // n_col, keep // n_band
    col_piece = lax.dynamic_slice_in_dim(plain, col * col_width, col_width, 1)

    def rows_of(other):
        return lax.dynamic_slice_in_dim(weighted, other * 2 * row_width, 2 * row_width, 1)

    pieces = [jnp.concatenate([col_piece, rows_of(group)], axis=1)]
    for mask in range(1, n_pair):
        pieces.append(swap(jnp.concatenate([col_piece, rows_of(group ^ mask)], axis=1), 2 * mask))
    gathered = jnp.concatenate(pieces)
    columns = gathered[:, :col_width]
    rows_low, rows_high = gathered[:, col_width : col_width + row_width], gathered[:, col_width + row_width :]
    rows_mine = jnp.where(side == 0, rows_low, rows_high)
    rows_other = jnp.where(side == 0, rows_high, rows_low)
    swapped = swap(jnp.concatenate([columns, rows_other], axis=1), 1)
    columns = jnp.concatenate([columns, swapped[:, :col_width]])
    rows = jnp.concatenate([rows_mine, swapped[:, col_width:]])
    response_tile = lax.dot_general(
        rows, columns, (((0,), (0,)), ((), ())), preferred_element_type=jnp.float32
    )
    factor = (rounds * band_local * n_band) ** (-0.5)
    return -response_tile * factor


def solution(mesh):
    return jax.shard_map(
        per_device,
        mesh=mesh,
        in_specs=(
            P("band", "col", None, None),
            P("band", "col", None, None),
            P(),
            P("band"),
            P(),
            P(),
        ),
        out_specs=P("band", "col"),
        check_vma=False,
    )
```

time: 272 us -> 131 us (0.48)
  local copies, waits for them, and re-layouts: 95 us -> 2.88 us
  Pallas kernels: 0 us -> 41.8 us
  blocking collectives: 29.9 us -> 0 us
  waiting for transfers between devices: 62.2 us -> 36.6 us
  other arithmetic: 39.3 us -> 16.1 us
  starting transfers between devices: 3.34 us -> 20.7 us
  matrix products: 18 us -> 0.94 us
  between operations: 21.3 us -> 11.5 us
    psum x1 -> x0, waiting for transfers between devices: 62.2 us -> none  [broadcast(): return lax.psum(jnp.where(mine, value, jnp.zeros_like(value)), axis)]
    reshape x3 -> x0, local copies, waits for them, and re-layouts: 57 us -> none  [per_device(): along_y.reshape(band_local, x_local, length * length)]
    pallas_call x0 -> x3, Pallas kernels: none -> 41.8 us  [round_coeffs(): pl.pallas_call(round_kernel, out_shape=jax.ShapeDtypeStruct((rows, keep),...]
    ppermute x0 -> x18, waiting for transfers between devices: none -> 36.6 us  [the longest x15 33.7 us: swap(): return lax.ppermute(value, 'band', [(i, i ^ mask) for i in range(n_band)])]
    reduce_sum x1 -> x0, other arithmetic: 28.2 us -> none  [per_device(): partial_list.append(jnp.sum(picked * table_x[None], axis=1) * norm_factor)]
    gather x3 -> x0, local copies, waits for them, and re-layouts: 28.1 us -> none  [per_device(): jnp.take(along_y.reshape(band_local, x_local, length * length), flat_inde...]
    ppermute x0 -> x18, starting transfers between devices: none -> 20.7 us  [the longest x15 15.1 us: swap(): return lax.ppermute(value, 'band', [(i, i ^ mask) for i in range(n_band)])]
    psum x1 -> x0, blocking collectives: 20.3 us -> none  [per_device(): coeffs = lax.psum(partial_all, 'col')]
  transfers between devices with their start and end apart: 2 -> 18, of which waited for: 1 -> 11; matrix products, arithmetic and copies ran while one was open for 2% -> 13% of each run, Pallas kernels for 0% -> 21%
where the time goes in v1:
time: 131 us
  Pallas kernels  41.8 us (32%)
  waiting for transfers between devices  36.6 us (28%)
  starting transfers between devices  20.7 us (16%)
  other arithmetic  16.1 us (12%)
  between operations  11.5 us (9%)
  local copies, waits for them, and re-layouts  2.88 us (2%)
    pallas_call x3, Pallas kernels, round_coeffs(): pl.pallas_call(round_kernel, out_shape=jax.ShapeDtypeStruct((rows, keep),...  41.8 us
    ppermute x15, waiting for transfers between devices, swap(): return lax.ppermute(value, 'band', [(i, i ^ mask) for i in range(n_band)])  33.7 us
    ppermute x15, starting transfers between devices, swap(): return lax.ppermute(value, 'band', [(i, i ^ mask) for i in range(n_band)])  15.1 us
    ppermute x3, starting transfers between devices, per_device(): lax.ppermute(sent, 'col', [(i, (i + shift) % n_col) for i in range(n_col)])  5.57 us
    select_n x2, other arithmetic, halves(): return (jnp.where(side == 0, low, high), jnp.where(side == 0, high, low))  3.32 us
    mul x1, other arithmetic, per_device(): cas_of(kept[0][:, None] * x_global[None, :] % length, length)  3.17 us
    ppermute x3, waiting for transfers between devices, per_device(): lax.ppermute(sent, 'col', [(i, (i + shift) % n_col) for i in range(n_col)])  2.91 us
  transfers between devices with their start and end apart: 18, of which 11 were waited for; matrix products, arithmetic and copies ran while one was open for 13% of the time, Pallas kernels for 21%

profile of v1, /device:TPU:0, one launch (start us, length us, event | category | flops | bytes accessed | tf_op | source)
XLA Modules:
  0.0 130.5 jit_solution(11915117283305002798)
XLA Ops:
  0.0 1.3 broadcast_select_fusion.5
  1.3 0.5 collective-permute-start
  1.8 2.0 %broadcast_select_fusion.2 = bf16[3,16,128,128]{3,2,1,0:T(8,128)(2,1)S(1)} fusion(pred[]{:T(512)S(6)} %eq.77, bf16[3,32,128,128]{3,2,1,0:T(8,128)(2,1)} %param.7), kind=kLoop, calls=%fused_computation.2 | loop fusion | flops 786432 | bytes 4718593 | tf_op jit(solution)/shard_map/jit(_where)/select_n | solution.py:114
  3.9 0.1 collective-permute-start.5
  4.1 0.7 fusion.25
  4.8 0.7 fusion.21
  5.5 0.8 pad_maximum_fusion.1
  6.4 3.0 %collective-permute-start.3 = (bf16[2,8,128,128]{3,2,1,0:T(8,128)(2,1)}, bf16[2,8,128,128]{3,2,1,0:T(8,128)(2,1)}, u32[]{:S(2)}, u32[]{:S(2)}) collective-permute-start(bf16[2,8,128,128]{3,2,1,0:T(8,128)(2,1)} %pad_maximum_fusion.1), channel_id=1, source_target_pairs={{0,16},{4,20},{8,24},{12,28},{16,0},{20,4},{24,8},{28,12},{1,17},{... | collective-permute-start | bytes 1572872 | tf_op jit(solution)/shard_map/ppermute | solution.py:110
  13.1 3.2 %add_multiply_fusion.tx_ref = f32[1536,128]{1,0:T(8,128)S(1)} fusion(s32[128]{0:T(128)S(1)} %fusion.17, s32[1536]{0:T(1024)S(1)} %get-tuple-element.5), kind=kLoop, calls=%fused_computation.14 | loop fusion | flops 3145728 | bytes 793088 | tf_op jit(solution)/shard_map/mul | solution.py:158
  16.2 5.6 %collective-permute-done.3 = bf16[2,8,128,128]{3,2,1,0:T(8,128)(2,1)} collective-permute-done((bf16[2,8,128,128]{3,2,1,0:T(8,128)(2,1)}, bf16[2,8,128,128]{3,2,1,0:T(8,128)(2,1)}, u32[]{:S(2)}, u32[]{:S(2)}) %collective-permute-start.3) | collective-permute-done | bytes 524320 | tf_op jit(solution)/shard_map/ppermute | solution.py:110
  21.8 2.1 %select_bitcast_fusion.4 = (bf16[8,128,128]{2,1,0:T(8,128)(2,1)}, bf16[8,128,128]{2,1,0:T(8,128)(2,1)}, bf16[8,128,128]{2,1,0:T(8,128)(2,1)}, bf16[1,8,128,128]{3,2,1,0:T(8,128)(2,1)}) fusion(pred[]{:T(512)} %bitcast, pred[]{:T(512)S(6)} %eq.82, bf16[2,8,128,128]{3,2,1,0:T(8,128)(2,1)} %collective-permute-done.3, ...), kind=kLoop, calls=%fused_computation.23 | loop fusion | flops 1179648 | bytes 2359302 | tf_op jit(solution)/shard_map/jit(_where)/select_n | solution.py:140
  23.9 1.7 %collective-permute-start.4 = (bf16[8,128,128]{2,1,0:T(8,128)(2,1)}, bf16[8,128,128]{2,1,0:T(8,128)(2,1)}, u32[]{:S(2)}, u32[]{:S(2)}) collective-permute-start(bf16[8,128,128]{2,1,0:T(8,128)(2,1)} %get-tuple-element.11), channel_id=1, source_target_pairs={{0,8},{4,12},{8,0},{12,4},{16,24},{20,28},{24,16},{28,20},{1,9},{5... | collective-permute-start | bytes 786440 | tf_op jit(solution)/shard_map/ppermute | solution.py:110
  25.6 0.6 fusion.28
  33.8 0.7 fusion.27
  34.5 0.3 add_convert_fusion.table_ref
  34.7 0.4 collective-permute-start.7
  35.1 1.1 pad_maximum_fusion
  36.2 1.8 %collective-permute-start.1 = (bf16[2,8,128,128]{3,2,1,0:T(8,128)(2,1)S(1)}, bf16[2,8,128,128]{3,2,1,0:T(8,128)(2,1)S(1)}, u32[]{:S(2)}, u32[]{:S(2)}) collective-permute-start(bf16[2,8,128,128]{3,2,1,0:T(8,128)(2,1)S(1)} %pad_maximum_fusion), channel_id=1, source_target_pairs={{0,8},{4,12},{8,0},{12,4},{16,24},{20,28},{24,16},{28,20},{1,9},{5... | collective-permute-start | bytes 1572872 | tf_op jit(solution)/shard_map/ppermute | solution.py:110
  38.0 0.3 collective-permute-start.9
  38.3 1.0 broadcast_select_fusion.10.vb_ref
  39.3 5.0 %collective-permute-done.7 = bf16[8,128,128]{2,1,0:T(8,128)(2,1)S(1)} collective-permute-done((bf16[8,128,128]{2,1,0:T(8,128)(2,1)}, bf16[8,128,128]{2,1,0:T(8,128)(2,1)S(1)}, u32[]{:S(2)}, u32[]{:S(2)}) %collective-permute-start.7) | collective-permute-done | bytes 262176 | tf_op jit(solution)/shard_map/ppermute | solution.py:110
  44.3 14.6 %collective-permute-done.9 = bf16[8,128,128]{2,1,0:T(8,128)(2,1)S(1)} collective-permute-done((bf16[8,128,128]{2,1,0:T(8,128)(2,1)}, bf16[8,128,128]{2,1,0:T(8,128)(2,1)S(1)}, u32[]{:S(2)}, u32[]{:S(2)}) %collective-permute-start.9) | collective-permute-done | bytes 262176 | tf_op jit(solution)/shard_map/ppermute | solution.py:110
  59.0 0.1 select_bitcast_fusion.5
  59.1 1.6 %collective-permute-start.2 = (bf16[8,128,128]{2,1,0:T(8,128)(2,1)S(1)}, bf16[8,128,128]{2,1,0:T(8,128)(2,1)S(1)}, u32[]{:S(2)}, u32[]{:S(2)}) collective-permute-start(bf16[8,128,128]{2,1,0:T(8,128)(2,1)S(1)} %get-tuple-element.14), channel_id=1, source_target_pairs={{0,16},{4,20},{8,24},{12,28},{16,0},{20,4},{24,8},{28,12},{1,17},{... | collective-permute-start | bytes 786440 | tf_op jit(solution)/shard_map/ppermute | solution.py:110
  60.7 0.5 collective-permute-start.6
  61.2 1.5 %collective-permute-start.8 = (bf16[8,128,128]{2,1,0:T(8,128)(2,1)S(1)}, bf16[8,128,128]{2,1,0:T(8,128)(2,1)S(1)}, u32[]{:S(2)}, u32[]{:S(2)}) collective-permute-start(bf16[8,128,128]{2,1,0:T(8,128)(2,1)S(1)} %get-tuple-element.15), channel_id=1, source_target_pairs={{0,16},{4,20},{8,24},{12,28},{16,0},{20,4},{24,8},{28,12},{1,17},{... | collective-permute-start | bytes 786440 | tf_op jit(solution)/shard_map/ppermute | solution.py:110
  62.7 1.7 %broadcast_select_fusion = (bf16[3,16,128,128]{3,2,1,0:T(8,128)(2,1)S(1)}, bf16[3,16,128,128]{3,2,1,0:T(8,128)(2,1)S(1)}) fusion(bf16[3,16,128,128]{3,2,1,0:T(8,128)(2,1)} %collective-permute-done.5, pred[]{:T(512)S(6)} %eq.77, bf16[3,32,128,128]{3,2,1,0:T(8,128)(2,1)S(1)} %copy-done), kind=kLoop, calls=%fused_computation | loop fusion | flops 2359296 | bytes 7864321 | tf_op jit(solution)/shard_map/jit(_where)/select_n | solution.py:121
  64.4 4.0 %collective-permute-done.2 = bf16[8,128,128]{2,1,0:T(8,128)(2,1)S(1)} collective-permute-done((bf16[8,128,128]{2,1,0:T(8,128)(2,1)S(1)}, bf16[8,128,128]{2,1,0:T(8,128)(2,1)S(1)}, u32[]{:S(2)}, u32[]{:S(2)}) %collective-permute-start.2) | collective-permute-done | bytes 262176 | tf_op jit(solution)/shard_map/ppermute | solution.py:110
  68.5 13.9 %round_coeffs.3 = f32[8,1536]{1,0:T(8,128)S(1)} custom-call(s32[1536]{0:T(1024)S(1)} %get-tuple-element.6.index_ref, bf16[8,128,128]{2,1,0:T(8,128)(2,1)S(1)} %broadcast_select_fusion.11.va_ref, bf16[8,128,128]{2,1,0:T(8,128)(2,1)S(1)} %broadcast_select_fusion.10.vb_ref, bf16[3,16,128,128]{3,2,1,0:T(8,128)(2,1)S(1)} %get-tuple-element.10.c0_ref, ...), custom_call_target="tpu_custom_call" | custom-call | flops 4000000000 | bytes 12582912 | tf_op jit(solution)/shard_map/round_coeffs/pallas_call | solution.py:79
  82.5 13.9 %round_coeffs.4 = f32[8,1536]{1,0:T(8,128)S(1)} custom-call(s32[1536]{0:T(1024)S(1)} %get-tuple-element.6.index_ref, bf16[8,128,128]{2,1,0:T(8,128)(2,1)S(1)} %broadcast_select_fusion.9.va_ref, bf16[8,128,128]{2,1,0:T(8,128)(2,1)S(1)} %broadcast_select_fusion.8.vb_ref, bf16[3,16,128,128]{3,2,1,0:T(8,128)(2,1)S(1)} %get-tuple-element.10.c0_ref, ...), custom_call_target="tpu_custom_call" | custom-call | flops 4000000000 | bytes 12582912 | tf_op jit(solution)/shard_map/round_coeffs/pallas_call | solution.py:79
  96.5 13.9 %round_coeffs.5 = f32[8,1536]{1,0:T(8,128)S(1)} custom-call(s32[1536]{0:T(1024)S(1)} %get-tuple-element.6.index_ref, bf16[8,128,128]{2,1,0:T(8,128)(2,1)S(1)} %broadcast_select_fusion.7.va_ref, bf16[8,128,128]{2,1,0:T(8,128)(2,1)S(1)} %broadcast_select_fusion.6.vb_ref, bf16[3,16,128,128]{3,2,1,0:T(8,128)(2,1)S(1)} %get-tuple-element.10.c0_ref, ...), custom_call_target="tpu_custom_call" | custom-call | flops 4000000000 | bytes 12582912 | tf_op jit(solution)/shard_map/round_coeffs/pallas_call | solution.py:79
  110.6 1.9 %subtract_divide_fusion.2 = (f32[3]{0:T(128)S(1)}, f32[3]{0:T(128)S(1)}, f32[3]{0:T(128)S(1)}) fusion(f32[3]{0:T(128)S(1)} %copy-done.6, f32[]{:T(128)} %bitcast.16, f32[]{:T(128)} %bitcast.20, f32[]{:T(128)} %bitcast.18), kind=kLoop, calls=%fused_computation.77 | loop fusion | flops 18 | bytes 60 | tf_op jit(solution)/shard_map/div | solution.py:171
  112.6 1.6 %collective-permute-start.11 = (bf16[9,1536]{1,0:T(8,128)(2,1)S(1)}, bf16[9,1536]{1,0:T(8,128)(2,1)S(1)}, u32[]{:S(2)}, u32[]{:S(2)}) collective-permute-start(bf16[9,1536]{1,0:T(8,128)(2,1)S(1)} %fusion.20), channel_id=1, source_target_pairs={{0,1},{1,2},{2,3},{3,0},{4,5},{5,6},{6,7},{7,4},{8,9},{9,10},{10,1... | collective-permute-start | bytes 82952 | tf_op jit(solution)/shard_map/ppermute | solution.py:169
  114.2 2.6 %collective-permute-start.12 = (bf16[9,1536]{1,0:T(8,128)(2,1)S(1)}, bf16[9,1536]{1,0:T(8,128)(2,1)S(1)}, u32[]{:S(2)}, u32[]{:S(2)}) collective-permute-start(bf16[9,1536]{1,0:T(8,128)(2,1)S(1)} %fusion.20), channel_id=1, source_target_pairs={{0,2},{1,3},{2,0},{3,1},{4,6},{5,7},{6,4},{7,5},{8,10},{9,11},{10,... | collective-permute-start | bytes 82952 | tf_op jit(solution)/shard_map/ppermute | solution.py:169
  116.8 1.3 %collective-permute-start.13 = (bf16[9,1536]{1,0:T(8,128)(2,1)S(1)}, bf16[9,1536]{1,0:T(8,128)(2,1)S(1)}, u32[]{:S(2)}, u32[]{:S(2)}) collective-permute-start(bf16[9,1536]{1,0:T(8,128)(2,1)S(1)} %fusion.20), channel_id=1, source_target_pairs={{0,3},{1,0},{2,1},{3,2},{4,7},{5,4},{6,5},{7,6},{8,11},{9,8},{10,9... | collective-permute-start | bytes 82952 | tf_op jit(solution)/shard_map/ppermute | solution.py:169
  118.2 0.5 collective-permute-done.11
  118.7 2.1 %collective-permute-done.12 = bf16[9,1536]{1,0:T(8,128)(2,1)S(1)} collective-permute-done((bf16[9,1536]{1,0:T(8,128)(2,1)S(1)}, bf16[9,1536]{1,0:T(8,128)(2,1)S(1)}, u32[]{:S(2)}, u32[]{:S(2)}) %collective-permute-start.12) | collective-permute-done | bytes 27680 | tf_op jit(solution)/shard_map/ppermute | solution.py:169
  120.8 0.3 collective-permute-done.13
  121.1 0.1 multiply_convert_fusion
  121.3 0.6 collective-permute-start.14
  121.9 1.5 %collective-permute-start.15 = (bf16[9,768]{1,0:T(8,128)(2,1)S(1)}, bf16[9,768]{1,0:T(8,128)(2,1)S(1)}, u32[]{:S(2)}, u32[]{:S(2)}) collective-permute-start(bf16[9,768]{1,0:T(8,128)(2,1)S(1)} %get-tuple-element.35), channel_id=1, source_target_pairs={{0,16},{4,20},{8,24},{12,28},{16,0},{20,4},{24,8},{28,12},{1,17},{... | collective-permute-start | bytes 41480 | tf_op jit(solution)/shard_map/ppermute | solution.py:110
  123.4 1.4 %collective-permute-start.16 = (bf16[9,768]{1,0:T(8,128)(2,1)S(1)}, bf16[9,768]{1,0:T(8,128)(2,1)S(1)}, u32[]{:S(2)}, u32[]{:S(2)}) collective-permute-start(bf16[9,768]{1,0:T(8,128)(2,1)S(1)} %get-tuple-element.36), channel_id=1, source_target_pairs={{0,24},{4,28},{8,16},{12,20},{16,8},{20,12},{24,0},{28,4},{1,25},{... | collective-permute-start | bytes 41480 | tf_op jit(solution)/shard_map/ppermute | solution.py:110
  124.9 0.5 collective-permute-done.14
  125.3 0.4 collective-permute-done.15
  125.7 2.4 %collective-permute-done.16 = bf16[9,768]{1,0:T(8,128)(2,1)S(1)} collective-permute-done((bf16[9,768]{1,0:T(8,128)(2,1)S(1)}, bf16[9,768]{1,0:T(8,128)(2,1)S(1)}, u32[]{:S(2)}, u32[]{:S(2)}) %collective-permute-start.16) | collective-permute-done | bytes 13856 | tf_op jit(solution)/shard_map/ppermute | solution.py:110
  128.2 0.1 broadcast_select_fusion.13
  128.4 1.2 collective-permute-done.17
  129.6 0.9 fusion
  (46 shorter events, 0.8 us)
Async XLA Ops:
  1.3 2.8 %copy-start.4 = (s32[3]{0:T(128)S(1)}, s32[3]{0:T(128)}, u32[]{:S(2)}) copy-start(s32[3]{0:T(128)} %param.11) | copy-start | bytes 40
  1.3 3.4 %copy-start.3 = (s32[3,1536]{1,0:T(4,128)S(1)}, s32[3,1536]{1,0:T(4,128)}, u32[]{:S(2)}) copy-start(s32[3,1536]{1,0:T(4,128)} %param.10) | copy-start | bytes 55300
  1.3 3.5 %collective-permute-start = (bf16[1,16,128,128]{3,2,1,0:T(8,128)(2,1)S(1)}, bf16[1,16,128,128]{3,2,1,0:T(8,128)(2,1)S(1)}, u32[]{:S(2)}, u32[]{:S(2)}) collective-permute-start(bf16[1,16,128,128]{3,2,1,0:T(8,128)(2,1)S(1)} %get-tuple-element.18), channel_id=1, source_target_pairs={{0,4},{4,0},{8,12},{12,8},{16,20},{20,16},{24,28},{28,24},{1,5},{5... | collective-permute-start | bytes 1572872 | tf_op jit(solution)/shard_map/ppermute | solution.py:110
  3.9 58.9 %collective-permute-start.5 = (bf16[3,16,128,128]{3,2,1,0:T(8,128)(2,1)S(1)}, bf16[3,16,128,128]{3,2,1,0:T(8,128)(2,1)}, u32[]{:S(2)}, u32[]{:S(2)}) collective-permute-start(bf16[3,16,128,128]{3,2,1,0:T(8,128)(2,1)S(1)} %broadcast_select_fusion.2), channel_id=1, source_target_pairs={{0,4},{4,0},{8,12},{12,8},{16,20},{20,16},{24,28},{28,24},{1,5},{5... | collective-permute-start | bytes 4718600 | tf_op jit(solution)/shard_map/ppermute | solution.py:110
  6.4 15.4 %collective-permute-start.3 = (bf16[2,8,128,128]{3,2,1,0:T(8,128)(2,1)}, bf16[2,8,128,128]{3,2,1,0:T(8,128)(2,1)}, u32[]{:S(2)}, u32[]{:S(2)}) collective-permute-start(bf16[2,8,128,128]{3,2,1,0:T(8,128)(2,1)} %pad_maximum_fusion.1), channel_id=1, source_target_pairs={{0,16},{4,20},{8,24},{12,28},{16,0},{20,4},{24,8},{28,12},{1,17},{... | collective-permute-start | bytes 1572872 | tf_op jit(solution)/shard_map/ppermute | solution.py:110
  13.0 20.7 %copy-start.5 = (f32[8]{0:T(128)S(1)}, f32[8]{0:T(128)}, u32[]{:S(2)}) copy-start(f32[8]{0:T(128)} %param.8) | copy-start | bytes 100
  23.9 14.4 %collective-permute-start.4 = (bf16[8,128,128]{2,1,0:T(8,128)(2,1)}, bf16[8,128,128]{2,1,0:T(8,128)(2,1)}, u32[]{:S(2)}, u32[]{:S(2)}) collective-permute-start(bf16[8,128,128]{2,1,0:T(8,128)(2,1)} %get-tuple-element.11), channel_id=1, source_target_pairs={{0,8},{4,12},{8,0},{12,4},{16,24},{20,28},{24,16},{28,20},{1,9},{5... | collective-permute-start | bytes 786440 | tf_op jit(solution)/shard_map/ppermute | solution.py:110
  33.8 10.5 %copy-start.2 = (bf16[8,128,128]{2,1,0:T(8,128)(2,1)S(1)}, bf16[8,128,128]{2,1,0:T(8,128)(2,1)}, u32[]{:S(2)}) copy-start(bf16[8,128,128]{2,1,0:T(8,128)(2,1)} %get-tuple-element.13) | copy-start | bytes 786436
  33.8 25.2 %copy-start.1 = (bf16[8,128,128]{2,1,0:T(8,128)(2,1)S(1)}, bf16[8,128,128]{2,1,0:T(8,128)(2,1)}, u32[]{:S(2)}) copy-start(bf16[8,128,128]{2,1,0:T(8,128)(2,1)} %get-tuple-element.12) | copy-start | bytes 786436
  34.7 9.6 %collective-permute-start.7 = (bf16[8,128,128]{2,1,0:T(8,128)(2,1)}, bf16[8,128,128]{2,1,0:T(8,128)(2,1)S(1)}, u32[]{:S(2)}, u32[]{:S(2)}) collective-permute-start(bf16[8,128,128]{2,1,0:T(8,128)(2,1)} %get-tuple-element.13), channel_id=1, source_target_pairs={{0,8},{4,12},{8,0},{12,4},{16,24},{20,28},{24,16},{28,20},{1,9},{5... | collective-permute-start | bytes 786440 | tf_op jit(solution)/shard_map/ppermute | solution.py:110
  36.2 22.8 %collective-permute-start.1 = (bf16[2,8,128,128]{3,2,1,0:T(8,128)(2,1)S(1)}, bf16[2,8,128,128]{3,2,1,0:T(8,128)(2,1)S(1)}, u32[]{:S(2)}, u32[]{:S(2)}) collective-permute-start(bf16[2,8,128,128]{3,2,1,0:T(8,128)(2,1)S(1)} %pad_maximum_fusion), channel_id=1, source_target_pairs={{0,8},{4,12},{8,0},{12,4},{16,24},{20,28},{24,16},{28,20},{1,9},{5... | collective-permute-start | bytes 1572872 | tf_op jit(solution)/shard_map/ppermute | solution.py:110
  38.0 21.0 %collective-permute-start.9 = (bf16[8,128,128]{2,1,0:T(8,128)(2,1)}, bf16[8,128,128]{2,1,0:T(8,128)(2,1)S(1)}, u32[]{:S(2)}, u32[]{:S(2)}) collective-permute-start(bf16[8,128,128]{2,1,0:T(8,128)(2,1)} %get-tuple-element.12), channel_id=1, source_target_pairs={{0,8},{4,12},{8,0},{12,4},{16,24},{20,28},{24,16},{28,20},{1,9},{5... | collective-permute-start | bytes 786440 | tf_op jit(solution)/shard_map/ppermute | solution.py:110
  44.3 18.4 %copy-start = (bf16[3,32,128,128]{3,2,1,0:T(8,128)(2,1)S(1)}, bf16[3,32,128,128]{3,2,1,0:T(8,128)(2,1)}, u32[]{:S(2)}) copy-start(bf16[3,32,128,128]{3,2,1,0:T(8,128)(2,1)} %param.7) | copy-start | bytes 9437188
  59.1 9.3 %collective-permute-start.2 = (bf16[8,128,128]{2,1,0:T(8,128)(2,1)S(1)}, bf16[8,128,128]{2,1,0:T(8,128)(2,1)S(1)}, u32[]{:S(2)}, u32[]{:S(2)}) collective-permute-start(bf16[8,128,128]{2,1,0:T(8,128)(2,1)S(1)} %get-tuple-element.14), channel_id=1, source_target_pairs={{0,16},{4,20},{8,24},{12,28},{16,0},{20,4},{24,8},{28,12},{1,17},{... | collective-permute-start | bytes 786440 | tf_op jit(solution)/shard_map/ppermute | solution.py:110
  60.7 21.7 %collective-permute-start.6 = (bf16[8,128,128]{2,1,0:T(8,128)(2,1)S(1)}, bf16[8,128,128]{2,1,0:T(8,128)(2,1)S(1)}, u32[]{:S(2)}, u32[]{:S(2)}) collective-permute-start(bf16[8,128,128]{2,1,0:T(8,128)(2,1)S(1)} %get-tuple-element.16), channel_id=1, source_target_pairs={{0,16},{4,20},{8,24},{12,28},{16,0},{20,4},{24,8},{28,12},{1,17},{... | collective-permute-start | bytes 786440 | tf_op jit(solution)/shard_map/ppermute | solution.py:110
  61.2 35.2 %collective-permute-start.8 = (bf16[8,128,128]{2,1,0:T(8,128)(2,1)S(1)}, bf16[8,128,128]{2,1,0:T(8,128)(2,1)S(1)}, u32[]{:S(2)}, u32[]{:S(2)}) collective-permute-start(bf16[8,128,128]{2,1,0:T(8,128)(2,1)S(1)} %get-tuple-element.15), channel_id=1, source_target_pairs={{0,16},{4,20},{8,24},{12,28},{16,0},{20,4},{24,8},{28,12},{1,17},{... | collective-permute-start | bytes 786440 | tf_op jit(solution)/shard_map/ppermute | solution.py:110
  96.5 14.1 %copy-start.6 = (f32[3]{0:T(128)S(1)}, f32[3]{0:T(128)}, u32[]{:S(2)}) copy-start(f32[3]{0:T(128)} %param.9) | copy-start | bytes 40
  110.5 2.0 %collective-permute-start.10 = (f32[9,1536]{1,0:T(8,128)S(1)}, f32[9,1536]{1,0:T(8,128)S(1)}, u32[]{:S(2)}, u32[]{:S(2)}) collective-permute-start(f32[9,1536]{1,0:T(8,128)S(1)} %fusion.4), channel_id=1, source_target_pairs={{0,4},{4,0},{8,12},{12,8},{16,20},{20,16},{24,28},{28,24},{1,5},{5... | collective-permute-start | bytes 165896 | tf_op jit(solution)/shard_map/ppermute | solution.py:110
  112.6 6.1 %collective-permute-start.11 = (bf16[9,1536]{1,0:T(8,128)(2,1)S(1)}, bf16[9,1536]{1,0:T(8,128)(2,1)S(1)}, u32[]{:S(2)}, u32[]{:S(2)}) collective-permute-start(bf16[9,1536]{1,0:T(8,128)(2,1)S(1)} %fusion.20), channel_id=1, source_target_pairs={{0,1},{1,2},{2,3},{3,0},{4,5},{5,6},{6,7},{7,4},{8,9},{9,10},{10,1... | collective-permute-start | bytes 82952 | tf_op jit(solution)/shard_map/ppermute | solution.py:169
  114.2 6.6 %collective-permute-start.12 = (bf16[9,1536]{1,0:T(8,128)(2,1)S(1)}, bf16[9,1536]{1,0:T(8,128)(2,1)S(1)}, u32[]{:S(2)}, u32[]{:S(2)}) collective-permute-start(bf16[9,1536]{1,0:T(8,128)(2,1)S(1)} %fusion.20), channel_id=1, source_target_pairs={{0,2},{1,3},{2,0},{3,1},{4,6},{5,7},{6,4},{7,5},{8,10},{9,11},{10,... | collective-permute-start | bytes 82952 | tf_op jit(solution)/shard_map/ppermute | solution.py:169
  116.8 4.3 %collective-permute-start.13 = (bf16[9,1536]{1,0:T(8,128)(2,1)S(1)}, bf16[9,1536]{1,0:T(8,128)(2,1)S(1)}, u32[]{:S(2)}, u32[]{:S(2)}) collective-permute-start(bf16[9,1536]{1,0:T(8,128)(2,1)S(1)} %fusion.20), channel_id=1, source_target_pairs={{0,3},{1,0},{2,1},{3,2},{4,7},{5,4},{6,5},{7,6},{8,11},{9,8},{10,9... | collective-permute-start | bytes 82952 | tf_op jit(solution)/shard_map/ppermute | solution.py:169
  121.3 4.0 %collective-permute-start.14 = (bf16[9,768]{1,0:T(8,128)(2,1)S(1)}, bf16[9,768]{1,0:T(8,128)(2,1)S(1)}, u32[]{:S(2)}, u32[]{:S(2)}) collective-permute-start(bf16[9,768]{1,0:T(8,128)(2,1)S(1)} %get-tuple-element.34), channel_id=1, source_target_pairs={{0,8},{4,12},{8,0},{12,4},{16,24},{20,28},{24,16},{28,20},{1,9},{5... | collective-permute-start | bytes 41480 | tf_op jit(solution)/shard_map/ppermute | solution.py:110
  121.9 3.8 %collective-permute-start.15 = (bf16[9,768]{1,0:T(8,128)(2,1)S(1)}, bf16[9,768]{1,0:T(8,128)(2,1)S(1)}, u32[]{:S(2)}, u32[]{:S(2)}) collective-permute-start(bf16[9,768]{1,0:T(8,128)(2,1)S(1)} %get-tuple-element.35), channel_id=1, source_target_pairs={{0,16},{4,20},{8,24},{12,28},{16,0},{20,4},{24,8},{28,12},{1,17},{... | collective-permute-start | bytes 41480 | tf_op jit(solution)/shard_map/ppermute | solution.py:110
  123.4 4.7 %collective-permute-start.16 = (bf16[9,768]{1,0:T(8,128)(2,1)S(1)}, bf16[9,768]{1,0:T(8,128)(2,1)S(1)}, u32[]{:S(2)}, u32[]{:S(2)}) collective-permute-start(bf16[9,768]{1,0:T(8,128)(2,1)S(1)} %get-tuple-element.36), channel_id=1, source_target_pairs={{0,24},{4,28},{8,16},{12,20},{16,8},{20,12},{24,0},{28,4},{1,25},{... | collective-permute-start | bytes 41480 | tf_op jit(solution)/shard_map/ppermute | solution.py:110
  128.3 1.3 collective-permute-start.17

commit v2 on v1

v2 whole, which is shorter than its diff:
```python
import jax
import jax.numpy as jnp
from jax import lax
from jax.experimental import pallas as pl
from jax.experimental.pallas import tpu as pltpu
from jax.sharding import PartitionSpec as P

LANES = 128
NT = (((1,), (1,)), ((), ()))


def cas_of(phase, length):
    angle_value = 2.0 * jnp.pi / length * phase.astype(jnp.float32)
    return jnp.cos(angle_value) + jnp.sin(angle_value)


def spaced_rows(used):
    tiles = -(-used // 8)
    return 8 * (tiles + 1 - tiles % 2)


def round_kernel(index_ref, va_ref, vb_ref, c0_ref, c1_ref, table_ref, tx_ref, out_ref, s_ref, a_ref, g_ref):
    length = va_ref.shape[1]
    bands = c0_ref.shape[0]
    planes = c0_ref.shape[1]
    keep, lanes = tx_ref.shape
    used = 2 * bands * planes
    spaced = spaced_rows(used)
    table = table_ref[...]

    def transform_z(c_ref, v_ref, band_base, x_base):
        half = v_ref.shape[0]
        steps = half // 2

        def step(i, carry):
            band, x = i // steps, (i % steps) * 2
            product = (v_ref[pl.ds(x, 2)] * c_ref[band, pl.ds(x + x_base, 2)]).reshape(2 * length, length)
            out = lax.dot_general(table, product, NT, preferred_element_type=jnp.float32)
            out = out.astype(jnp.bfloat16).astype(jnp.float32)
            row = (band_base + band) * planes + x + x_base
            s_ref[pl.ds(row, length, stride=spaced), :] = out[:, :length]
            s_ref[pl.ds(row + 1, length, stride=spaced), :] = out[:, length:]
            return carry

        lax.fori_loop(0, bands * steps, step, 0, unroll=bands * steps)

    for c_ref, band_base in ((c0_ref, 0), (c1_ref, bands)):
        transform_z(c_ref, va_ref, band_base, 0)
        transform_z(c_ref, vb_ref, band_base, va_ref.shape[0])

    def transform_y(j, carry):
        base = pl.multiple_of(j * 2 * spaced, 8)
        rows = jnp.concatenate([s_ref[pl.ds(base, lanes), :], s_ref[pl.ds(base + spaced, lanes), :]])
        out = lax.dot_general(table, rows.astype(jnp.bfloat16), NT, preferred_element_type=jnp.float32)
        base = pl.multiple_of(j * 2 * length, 2 * length)
        a_ref[pl.ds(base, length), :] = out[:, :lanes]
        a_ref[pl.ds(base + length, length), :] = out[:, lanes:]
        return carry

    lax.fori_loop(0, length // 2, transform_y, 0, unroll=16)

    def pick(t, carry):
        rows = [a_ref[pl.ds(index_ref[t * 8 + k], 1), :] for k in range(8)]
        g_ref[pl.ds(pl.multiple_of(t * 8, 8), 8), :] = jnp.concatenate(rows)
        return carry

    lax.fori_loop(0, keep // 8, pick, 0, unroll=8)

    lane = lax.broadcasted_iota(jnp.int32, (keep, lanes), 1)
    scaled = jnp.where(lane < used, g_ref[...] * tx_ref[...], 0.0)
    high = scaled.astype(jnp.bfloat16)
    low = (scaled - high.astype(jnp.float32)).astype(jnp.bfloat16)
    rows = out_ref.shape[0]
    owner = lax.broadcasted_iota(jnp.int32, (rows, lanes), 1) // planes
    select = (owner == lax.broadcasted_iota(jnp.int32, (rows, lanes), 0)).astype(jnp.bfloat16)
    out_ref[...] = lax.dot_general(select, high, NT, preferred_element_type=jnp.float32) + lax.dot_general(
        select, low, NT, preferred_element_type=jnp.float32
    )


def round_coeffs(index, va, vb, c0, c1, table, tx):
    keep, lanes = tx.shape
    length = table.shape[0]
    rows = -(-2 * c0.shape[0] // 8) * 8
    vmem = pl.BlockSpec(memory_space=pltpu.VMEM)
    return pl.pallas_call(
        round_kernel,
        out_shape=jax.ShapeDtypeStruct((rows, keep), jnp.float32),
        in_specs=[pl.BlockSpec(memory_space=pltpu.SMEM)] + [vmem] * 6,
        out_specs=vmem,
        scratch_shapes=[
            pltpu.VMEM((length * spaced_rows(2 * c0.shape[0] * c0.shape[1]) + lanes, length), jnp.float32),
            pltpu.VMEM((length * length, lanes), jnp.float32),
            pltpu.VMEM((keep, lanes), jnp.float32),
        ],
        compiler_params=pltpu.CompilerParams(vmem_limit_bytes=32 * 2**20),
        cost_estimate=pl.CostEstimate(flops=4 * 10**9, bytes_accessed=12 * 2**20, transcendentals=0),
        name="round_coeffs",
    )(index, va, vb, c0, c1, table, tx)


def per_device(valence, conduction, energy_val, energy_cond, kept, plan):
    band_local, x_local, length = conduction.shape[:3]
    keep = kept.shape[1]
    held = valence.shape[0]
    rounds = plan.shape[0]
    n_band = lax.axis_size("band")
    n_col = lax.axis_size("col")
    n_pair = n_band // 2
    bits = n_pair.bit_length() - 1
    me = lax.axis_index("band")
    side, group = me % 2, me // 2
    col = lax.axis_index("col")
    x_half = x_local // 2

    def swap(value, mask):
        return lax.ppermute(value, "band", [(i, i ^ mask) for i in range(n_band)])

    def half_of(value, which):
        return lax.dynamic_slice_in_dim(value, which * x_half, x_half, 1)

    v_mine = half_of(valence, side)
    v_swapped = swap(half_of(valence, 1 - side), 1)
    c_mine = half_of(conduction, side)
    c_swapped = swap(half_of(conduction, 1 - side), 1)

    position = jnp.arange(length, dtype=jnp.int32)
    table = cas_of(position[:, None] * position[None, :] % length, length).astype(jnp.bfloat16)
    used = 2 * band_local * x_half
    lanes = -(-used // LANES) * LANES
    x_global = col * x_local + side * x_half + jnp.arange(lanes, dtype=jnp.int32) % x_half
    tx = cas_of(kept[0][:, None] * x_global[None, :] % length, length) * length ** (-1.5)
    index = kept[2] * length + kept[1]

    is_target = plan[:, None] == jnp.arange(energy_val.shape[0], dtype=jnp.int32)[None, :]
    target_energy = jnp.sum(jnp.where(is_target, energy_val[None, :], 0.0), axis=1)
    weights = (1.0 / (energy_cond[None, :] - target_energy[:, None])).reshape(rounds * band_local, 1)

    plan_rows = jnp.broadcast_to(plan[:, None, None, None], (rounds, 1, 1, length))
    root = plan_rows // held
    local = plan_rows % held
    relative = (root // 2) ^ group
    near_side = root % 2 == side

    def held_band(mine, swapped, r):
        band = jnp.where(near_side[r], mine[0], swapped[0])
        for i in range(1, held):
            band = jnp.where(local[r] == i, jnp.where(near_side[r], mine[i], swapped[i]), band)
        return band

    def nearer(r, bit, near, far):
        return jnp.where((relative[r] >> bit) & 1 == 0, near, far)

    cut = x_half // 2
    parts = [(v_mine[:, :cut], v_swapped[:, :cut]), (v_mine[:, cut:], v_swapped[:, cut:])]
    orders = [list(range(bits)), list(range(bits))[::-1]]
    if 2 * held <= rounds and bits:
        far_mine = [swap(part[0], 2 << order[0]) for part, order in zip(parts, orders)]
        far_swapped = [swap(part[1], 2 << order[0]) for part, order in zip(parts, orders)]
        far_mine, far_swapped, c_swapped, table, tx, index, weights = lax.optimization_barrier(
            (far_mine, far_swapped, c_swapped, table, tx, index, weights)
        )
        slots = [
            [nearer(r, order[0], held_band(*part, r), held_band(fm, fs, r)) for part, fm, fs, order in zip(parts, far_mine, far_swapped, orders)]
            for r in range(rounds)
        ]
        slots = lax.optimization_barrier(slots)
        orders = [order[1:] for order in orders]
    else:
        slots = [[held_band(*part, r) for part in parts] for r in range(rounds)]
    for step in range(len(orders[0])):
        slots = [
            [nearer(r, order[step], value, swap(value, 2 << order[step])) for value, order in zip(slots[r], orders)]
            for r in range(rounds)
        ]

    c0 = jnp.where(side == 0, c_mine, c_swapped)
    c1 = jnp.where(side == 0, c_swapped, c_mine)

    partial = [round_coeffs(index, *slots[r], c0, c1, table, tx) for r in range(rounds)]

    first = jnp.concatenate([p[:band_local] for p in partial])
    second = jnp.concatenate([p[band_local : 2 * band_local] for p in partial])
    mine = jnp.where(side == 0, first, second)
    coeffs = mine + swap(jnp.where(side == 0, second, first), 1)
    sent = coeffs.astype(jnp.bfloat16)
    for shift in range(1, n_col):
        moved = lax.ppermute(sent, "col", [(i, (i + shift) % n_col) for i in range(n_col)])
        coeffs = coeffs + moved.astype(jnp.float32)
    weighted = (weights * coeffs).astype(jnp.bfloat16)
    plain = coeffs.astype(jnp.bfloat16)

    col_width, row_width = keep // n_col, keep // n_band
    col_piece = lax.dynamic_slice_in_dim(plain, col * col_width, col_width, 1)

    def rows_of(other):
        return lax.dynamic_slice_in_dim(weighted, other * 2 * row_width, 2 * row_width, 1)

    pieces = [jnp.concatenate([col_piece, rows_of(group)], axis=1)]
    for mask in range(1, n_pair):
        pieces.append(swap(jnp.concatenate([col_piece, rows_of(group ^ mask)], axis=1), 2 * mask))
    gathered = jnp.concatenate(pieces)
    columns = gathered[:, :col_width]
    rows_low, rows_high = gathered[:, col_width : col_width + row_width], gathered[:, col_width + row_width :]
    rows_mine = jnp.where(side == 0, rows_low, rows_high)
    rows_other = jnp.where(side == 0, rows_high, rows_low)
    swapped = swap(jnp.concatenate([columns, rows_other], axis=1), 1)
    columns = jnp.concatenate([columns, swapped[:, :col_width]])
    rows = jnp.concatenate([rows_mine, swapped[:, col_width:]])
    response_tile = lax.dot_general(
        rows, columns, (((0,), (0,)), ((), ())), preferred_element_type=jnp.float32
    )
    factor = (rounds * band_local * n_band) ** (-0.5)
    return -response_tile * factor


def solution(mesh):
    return jax.shard_map(
        per_device,
        mesh=mesh,
        in_specs=(
            P("band", "col", None, None),
            P("band", "col", None, None),
            P(),
            P("band"),
            P(),
            P(),
        ),
        out_specs=P("band", "col"),
        check_vma=False,
    )
```

time: 131 us -> 74.3 us (0.57)
  Pallas kernels: 41.8 us -> 17 us
  waiting for transfers between devices: 36.6 us -> 21.8 us
  between operations: 11.5 us -> 0.31 us
  other arithmetic: 16.1 us -> 8.49 us
  local copies, waits for them, and re-layouts: 2.88 us -> 5.52 us
    pallas_call x3, Pallas kernels: 41.8 us -> 17 us  [round_coeffs(): pl.pallas_call(round_kernel, out_shape=jax.ShapeDtypeStruct((rows, keep),...]
    ppermute x15 -> x17, waiting for transfers between devices: 33.7 us -> 16.9 us  [swap(): return lax.ppermute(value, 'band', [(i, i ^ mask) for i in range(n_band)])]
    select_n x10 -> x8, other arithmetic: 6.68 us -> 2.59 us  [nearer(): return jnp.where(relative[r] >> bit & 1 == 0, near, far)]
    dynamic_slice x1 -> x2, local copies, waits for them, and re-layouts: 0.66 us -> 3.4 us  [half_of(): return lax.dynamic_slice_in_dim(value, which * x_half, x_half, 1)]
    concatenate x3 -> x0, other arithmetic: 2 us -> none  [the longest x2 1.93 us: spread(): jnp.concatenate([mine, swapped])]
    ppermute x3, waiting for transfers between devices: 2.91 us -> 4.89 us  [per_device(): lax.ppermute(sent, 'col', [(i, (i + shift) % n_col) for i in range(n_col)])]
    div x1, other arithmetic: 1.87 us -> 0.07 us  [per_device(): 1.0 / (energy_cond[None, :] - target_energy[:, None])]
    ppermute x15 -> x17, starting transfers between devices: 15.1 us -> 15.4 us  [swap(): return lax.ppermute(value, 'band', [(i, i ^ mask) for i in range(n_band)])]
  transfers between devices with their start and end apart: 18 -> 20, of which waited for: 11 -> 12; matrix products, arithmetic and copies ran while one was open for 13% -> 14% of each run, Pallas kernels for 21% -> 15%
where the time goes in v2:
time: 74.3 us; the launch traced here: 74.1 us
  waiting for transfers between devices  21.8 us (29%)
  starting transfers between devices  20 us (27%)
  Pallas kernels  17 us (23%)
  other arithmetic  8.49 us (11%)
  local copies, waits for them, and re-layouts  5.52 us (7%)
  matrix products  0.94 us (1%)
    pallas_call x3, Pallas kernels, round_coeffs(): pl.pallas_call(round_kernel, out_shape=jax.ShapeDtypeStruct((rows, keep),...  17 us
    ppermute x17, waiting for transfers between devices, swap(): return lax.ppermute(value, 'band', [(i, i ^ mask) for i in range(n_band)])  16.9 us
    ppermute x17, starting transfers between devices, swap(): return lax.ppermute(value, 'band', [(i, i ^ mask) for i in range(n_band)])  15.4 us
    ppermute x3, waiting for transfers between devices, per_device(): lax.ppermute(sent, 'col', [(i, (i + shift) % n_col) for i in range(n_col)])  4.89 us
    ppermute x3, starting transfers between devices, per_device(): lax.ppermute(sent, 'col', [(i, (i + shift) % n_col) for i in range(n_col)])  4.66 us
    dynamic_slice x2, local copies, waits for them, and re-layouts, half_of(): return lax.dynamic_slice_in_dim(value, which * x_half, x_half, 1)  3.4 us
    mul x1, other arithmetic, per_device(): cas_of(kept[0][:, None] * x_global[None, :] % length, length)  3.17 us
    select_n x8, other arithmetic, nearer(): return jnp.where(relative[r] >> bit & 1 == 0, near, far)  2.59 us
  transfers between devices with their start and end apart: 20, of which 12 were waited for; matrix products, arithmetic and copies ran while one was open for 14% of the time, Pallas kernels for 15%

profile of v2, /device:TPU:0, one launch (start us, length us, event | category | flops | bytes accessed | tf_op | source)
XLA Modules:
  0.0 74.1 jit_solution(11204956933535548921)
XLA Ops:
  0.0 1.1 %constant_dynamic-slice_fusion.7 = (bf16[1,8,128,128]{3,2,1,0:T(8,128)(2,1)S(1)}, bf16[1,8,128,128]{3,2,1,0:T(8,128)(2,1)S(1)}) fusion(bf16[1,32,128,128]{3,2,1,0:T(8,128)(2,1)} %param.6, s32[]{:T(128)S(6)} %add.132, s32[]{:T(128)S(6)} %select_n.204), kind=kLoop, calls=%fused_computation.81 | loop fusion | bytes 1048584 | tf_op jit(solution)/shard_map/slice | solution.py:155
  1.1 3.0 %collective-permute-start.1 = (bf16[1,8,128,128]{3,2,1,0:T(8,128)(2,1)S(1)}, bf16[1,8,128,128]{3,2,1,0:T(8,128)(2,1)}, u32[]{:S(2)}, u32[]{:S(2)}) collective-permute-start(bf16[1,8,128,128]{3,2,1,0:T(8,128)(2,1)S(1)} %get-tuple-element.49), channel_id=1, source_target_pairs={{0,16},{4,20},{8,24},{12,28},{16,0},{20,4},{24,8},{28,12},{1,17},{... | collective-permute-start | bytes 786440 | tf_op jit(solution)/shard_map/ppermute | solution.py:117
  4.1 1.5 %collective-permute-start = (bf16[1,8,128,128]{3,2,1,0:T(8,128)(2,1)S(1)}, bf16[1,8,128,128]{3,2,1,0:T(8,128)(2,1)}, u32[]{:S(2)}, u32[]{:S(2)}) collective-permute-start(bf16[1,8,128,128]{3,2,1,0:T(8,128)(2,1)S(1)} %get-tuple-element.50), channel_id=1, source_target_pairs={{0,8},{4,12},{8,0},{12,4},{16,24},{20,28},{24,16},{28,20},{1,9},{5... | collective-permute-start | bytes 786440 | tf_op jit(solution)/shard_map/ppermute | solution.py:117
  5.6 1.9 %constant_dynamic-slice_fusion.6 = bf16[1,16,128,128]{3,2,1,0:T(8,128)(2,1)} fusion(bf16[1,32,128,128]{3,2,1,0:T(8,128)(2,1)} %param.6, s32[]{:T(128)S(6)} %select_n.205), kind=kLoop, calls=%fused_computation.80 | loop fusion | bytes 1048580 | tf_op jit(solution)/shard_map/dynamic_slice | solution.py:120
  7.6 1.5 %constant_dynamic-slice_fusion.5 = bf16[3,16,128,128]{3,2,1,0:T(8,128)(2,1)S(1)} fusion(bf16[3,32,128,128]{3,2,1,0:T(8,128)(2,1)} %param.7, s32[]{:T(128)S(6)} %select_n.205), kind=kLoop, calls=%fused_computation.79 | loop fusion | bytes 3145732 | tf_op jit(solution)/shard_map/dynamic_slice | solution.py:120
  9.1 0.6 collective-permute-start.5
  9.7 0.2 select_reduce_fusion
  9.9 0.1 subtract_divide_fusion
  10.0 0.1 fusion.23
  10.1 0.1 fusion.24
  10.2 3.2 %add_multiply_fusion.tx_ref = f32[1536,128]{1,0:T(8,128)S(1)} fusion(s32[128]{0:T(128)S(1)} %fusion.25, s32[1536]{0:T(1024)S(1)} %get-tuple-element.36), kind=kLoop, calls=%fused_computation.12 | loop fusion | flops 3145728 | bytes 793088 | tf_op jit(solution)/shard_map/mul | solution.py:132
  13.4 0.8 %fusion.28 = (bf16[1,8,128,128]{3,2,1,0:T(8,128)(2,1)}, bf16[1,8,128,128]{3,2,1,0:T(8,128)(2,1)}) fusion(bf16[1,16,128,128]{3,2,1,0:T(8,128)(2,1)S(1)} %collective-permute-done.2), kind=kLoop, calls=%fused_computation.105 | loop fusion | bytes 1048576 | tf_op jit(solution)/shard_map/slice | solution.py:155
  14.2 0.5 collective-permute-start.4
  14.7 0.1 collective-permute-start.3
  14.8 0.3 add_convert_fusion.table_ref
  15.1 0.1 div.35
  15.2 7.6 %collective-permute-done.4 = bf16[1,8,128,128]{3,2,1,0:T(8,128)(2,1)} collective-permute-done((bf16[1,8,128,128]{3,2,1,0:T(8,128)(2,1)}, bf16[1,8,128,128]{3,2,1,0:T(8,128)(2,1)}, u32[]{:S(2)}, u32[]{:S(2)}) %collective-permute-start.4) | collective-permute-done | bytes 262176 | tf_op jit(solution)/shard_map/ppermute | solution.py:117
  22.8 0.2 collective-permute-done.3
  23.0 1.3 %fusion.9 = (bf16[8,128,128]{2,1,0:T(8,128)(2,1)S(1)}, bf16[8,128,128]{2,1,0:T(8,128)(2,1)S(1)}, bf16[8,128,128]{2,1,0:T(8,128)(2,1)S(1)}) fusion(bf16[1,8,128,128]{3,2,1,0:T(8,128)(2,1)} %collective-permute-done.3, bf16[1,8,128,128]{3,2,1,0:T(8,128)(2,1)} %collective-permute-done, bf16[1,8,128,128]{3,2,1,0:T(8,128)(2,1)S(1)} %get-tuple-element.50, ...), kind=kLoop, calls=%fused_computation.27 | loop fusion | flops 1179648 | bytes 1835776 | tf_op jit(solution)/shard_map/jit(_where)/select_n | solution.py:152
  24.3 1.1 %fusion.6 = (bf16[8,128,128]{2,1,0:T(8,128)(2,1)S(1)}, bf16[8,128,128]{2,1,0:T(8,128)(2,1)S(1)}, bf16[8,128,128]{2,1,0:T(8,128)(2,1)S(1)}) fusion(bf16[1,8,128,128]{3,2,1,0:T(8,128)(2,1)} %collective-permute-done.4, bf16[1,8,128,128]{3,2,1,0:T(8,128)(2,1)} %collective-permute-done.1, bf16[1,8,128,128]{3,2,1,0:T(8,128)(2,1)S(1)} %get-tuple-element.49, ...), kind=kLoop, calls=%fused_computation.18 | loop fusion | flops 1179648 | bytes 1835776 | tf_op jit(solution)/shard_map/jit(_where)/select_n | solution.py:152
  25.4 1.6 %collective-permute-start.6 = (bf16[8,128,128]{2,1,0:T(8,128)(2,1)S(1)}, bf16[8,128,128]{2,1,0:T(8,128)(2,1)S(1)}, u32[]{:S(2)}, u32[]{:S(2)}) collective-permute-start(bf16[8,128,128]{2,1,0:T(8,128)(2,1)S(1)} %get-tuple-element.25), channel_id=1, source_target_pairs={{0,16},{4,20},{8,24},{12,28},{16,0},{20,4},{24,8},{28,12},{1,17},{... | collective-permute-start | bytes 786440 | tf_op jit(solution)/shard_map/ppermute | solution.py:117
  27.0 0.5 collective-permute-start.7
  27.6 0.3 collective-permute-start.8
  27.9 1.7 %collective-permute-start.9 = (bf16[8,128,128]{2,1,0:T(8,128)(2,1)S(1)}, bf16[8,128,128]{2,1,0:T(8,128)(2,1)S(1)}, u32[]{:S(2)}, u32[]{:S(2)}) collective-permute-start(bf16[8,128,128]{2,1,0:T(8,128)(2,1)S(1)} %get-tuple-element.31), channel_id=1, source_target_pairs={{0,8},{4,12},{8,0},{12,4},{16,24},{20,28},{24,16},{28,20},{1,9},{5... | collective-permute-start | bytes 786440 | tf_op jit(solution)/shard_map/ppermute | solution.py:117
  29.6 1.5 %collective-permute-start.10 = (bf16[8,128,128]{2,1,0:T(8,128)(2,1)S(1)}, bf16[8,128,128]{2,1,0:T(8,128)(2,1)S(1)}, u32[]{:S(2)}, u32[]{:S(2)}) collective-permute-start(bf16[8,128,128]{2,1,0:T(8,128)(2,1)S(1)} %get-tuple-element.32), channel_id=1, source_target_pairs={{0,16},{4,20},{8,24},{12,28},{16,0},{20,4},{24,8},{28,12},{1,17},{... | collective-permute-start | bytes 786440 | tf_op jit(solution)/shard_map/ppermute | solution.py:117
  31.1 1.6 %broadcast_select_fusion = (bf16[3,16,128,128]{3,2,1,0:T(8,128)(2,1)S(1)}, bf16[3,16,128,128]{3,2,1,0:T(8,128)(2,1)S(1)}) fusion(bf16[3,16,128,128]{3,2,1,0:T(8,128)(2,1)} %collective-permute-done.5, pred[]{:T(512)S(6)} %eq.117, bf16[3,32,128,128]{3,2,1,0:T(8,128)(2,1)S(1)} %copy-done, s32[]{:T(128)S(6)} %select_n.204), kind=kLoop, calls=%fused_computation | loop fusion | flops 1572864 | bytes 6291461 | tf_op jit(solution)/shard_map/jit(_where)/select_n | solution.py:178
  32.7 2.1 %collective-permute-done.6 = bf16[8,128,128]{2,1,0:T(8,128)(2,1)S(1)} collective-permute-done((bf16[8,128,128]{2,1,0:T(8,128)(2,1)S(1)}, bf16[8,128,128]{2,1,0:T(8,128)(2,1)S(1)}, u32[]{:S(2)}, u32[]{:S(2)}) %collective-permute-start.6) | collective-permute-done | bytes 262176 | tf_op jit(solution)/shard_map/ppermute | solution.py:117
  34.8 0.3 collective-permute-start.11
  35.1 1.2 %collective-permute-done.7 = bf16[8,128,128]{2,1,0:T(8,128)(2,1)S(1)} collective-permute-done((bf16[8,128,128]{2,1,0:T(8,128)(2,1)S(1)}, bf16[8,128,128]{2,1,0:T(8,128)(2,1)S(1)}, u32[]{:S(2)}, u32[]{:S(2)}) %collective-permute-start.7) | collective-permute-done | bytes 262176 | tf_op jit(solution)/shard_map/ppermute | solution.py:117
  36.3 5.8 %round_coeffs.3 = f32[8,1536]{1,0:T(8,128)S(1)} custom-call(s32[1536]{0:T(1024)S(1)} %get-tuple-element.20.index_ref, bf16[8,128,128]{2,1,0:T(8,128)(2,1)S(1)} %broadcast_select_fusion.7.va_ref, bf16[8,128,128]{2,1,0:T(8,128)(2,1)S(1)} %broadcast_select_fusion.6.vb_ref, bf16[3,16,128,128]{3,2,1,0:T(8,128)(2,1)S(1)} %get-tuple-element.42.c0_ref, ...), custom_call_target="tpu_custom_call" | custom-call | flops 4000000000 | bytes 12582912 | tf_op jit(solution)/shard_map/round_coeffs/pallas_call | solution.py:86
  42.2 5.6 %round_coeffs.4 = f32[8,1536]{1,0:T(8,128)S(1)} custom-call(s32[1536]{0:T(1024)S(1)} %get-tuple-element.20.index_ref, bf16[8,128,128]{2,1,0:T(8,128)(2,1)S(1)} %broadcast_select_fusion.4.va_ref, bf16[8,128,128]{2,1,0:T(8,128)(2,1)S(1)} %broadcast_select_fusion.5.vb_ref, bf16[3,16,128,128]{3,2,1,0:T(8,128)(2,1)S(1)} %get-tuple-element.42.c0_ref, ...), custom_call_target="tpu_custom_call" | custom-call | flops 4000000000 | bytes 12582912 | tf_op jit(solution)/shard_map/round_coeffs/pallas_call | solution.py:86
  48.0 5.6 %round_coeffs.5 = f32[8,1536]{1,0:T(8,128)S(1)} custom-call(s32[1536]{0:T(1024)S(1)} %get-tuple-element.20.index_ref, bf16[8,128,128]{2,1,0:T(8,128)(2,1)S(1)} %broadcast_select_fusion.2.va_ref, bf16[8,128,128]{2,1,0:T(8,128)(2,1)S(1)} %broadcast_select_fusion.3.vb_ref, bf16[3,16,128,128]{3,2,1,0:T(8,128)(2,1)S(1)} %get-tuple-element.42.c0_ref, ...), custom_call_target="tpu_custom_call" | custom-call | flops 4000000000 | bytes 12582912 | tf_op jit(solution)/shard_map/round_coeffs/pallas_call | solution.py:86
  53.7 1.3 %collective-permute-done.12 = f32[9,1536]{1,0:T(8,128)S(1)} collective-permute-done((f32[9,1536]{1,0:T(8,128)S(1)}, f32[9,1536]{1,0:T(8,128)S(1)}, u32[]{:S(2)}, u32[]{:S(2)}) %collective-permute-start.12) | collective-permute-done | bytes 55328 | tf_op jit(solution)/shard_map/ppermute | solution.py:117
  55.1 3.7 %collective-permute-start.15 = (bf16[9,1536]{1,0:T(8,128)(2,1)S(1)}, bf16[9,1536]{1,0:T(8,128)(2,1)S(1)}, u32[]{:S(2)}, u32[]{:S(2)}) collective-permute-start(bf16[9,1536]{1,0:T(8,128)(2,1)S(1)} %fusion.27), channel_id=1, source_target_pairs={{0,3},{1,0},{2,1},{3,2},{4,7},{5,4},{6,5},{7,6},{8,11},{9,8},{10,9... | collective-permute-start | bytes 82952 | tf_op jit(solution)/shard_map/ppermute | solution.py:188
  58.8 1.0 %collective-permute-start.13 = (bf16[9,1536]{1,0:T(8,128)(2,1)S(1)}, bf16[9,1536]{1,0:T(8,128)(2,1)S(1)}, u32[]{:S(2)}, u32[]{:S(2)}) collective-permute-start(bf16[9,1536]{1,0:T(8,128)(2,1)S(1)} %fusion.27), channel_id=1, source_target_pairs={{0,1},{1,2},{2,3},{3,0},{4,5},{5,6},{6,7},{7,4},{8,9},{9,10},{10,1... | collective-permute-start | bytes 82952 | tf_op jit(solution)/shard_map/ppermute | solution.py:188
  59.8 1.1 %collective-permute-done.15 = bf16[9,1536]{1,0:T(8,128)(2,1)S(1)} collective-permute-done((bf16[9,1536]{1,0:T(8,128)(2,1)S(1)}, bf16[9,1536]{1,0:T(8,128)(2,1)S(1)}, u32[]{:S(2)}, u32[]{:S(2)}) %collective-permute-start.15) | collective-permute-done | bytes 27680 | tf_op jit(solution)/shard_map/ppermute | solution.py:188
  60.9 3.2 %collective-permute-done.14 = bf16[9,1536]{1,0:T(8,128)(2,1)S(1)} collective-permute-done((bf16[9,1536]{1,0:T(8,128)(2,1)S(1)}, bf16[9,1536]{1,0:T(8,128)(2,1)S(1)}, u32[]{:S(2)}, u32[]{:S(2)}) %collective-permute-start.14) | collective-permute-done | bytes 27680 | tf_op jit(solution)/shard_map/ppermute | solution.py:188
  64.1 0.6 collective-permute-done.13
  64.7 0.1 multiply_convert_fusion
  64.8 0.6 collective-permute-start.16
  65.5 1.5 %collective-permute-start.17 = (bf16[9,768]{1,0:T(8,128)(2,1)S(1)}, bf16[9,768]{1,0:T(8,128)(2,1)S(1)}, u32[]{:S(2)}, u32[]{:S(2)}) collective-permute-start(bf16[9,768]{1,0:T(8,128)(2,1)S(1)} %get-tuple-element.66), channel_id=1, source_target_pairs={{0,16},{4,20},{8,24},{12,28},{16,0},{20,4},{24,8},{28,12},{1,17},{... | collective-permute-start | bytes 41480 | tf_op jit(solution)/shard_map/ppermute | solution.py:117
  66.9 1.4 %collective-permute-start.18 = (bf16[9,768]{1,0:T(8,128)(2,1)S(1)}, bf16[9,768]{1,0:T(8,128)(2,1)S(1)}, u32[]{:S(2)}, u32[]{:S(2)}) collective-permute-start(bf16[9,768]{1,0:T(8,128)(2,1)S(1)} %get-tuple-element.67), channel_id=1, source_target_pairs={{0,24},{4,28},{8,16},{12,20},{16,8},{20,12},{24,0},{28,4},{1,25},{... | collective-permute-start | bytes 41480 | tf_op jit(solution)/shard_map/ppermute | solution.py:117
  68.4 0.3 collective-permute-done.16
  68.7 0.6 collective-permute-done.17
  69.3 2.4 %collective-permute-done.18 = bf16[9,768]{1,0:T(8,128)(2,1)S(1)} collective-permute-done((bf16[9,768]{1,0:T(8,128)(2,1)S(1)}, bf16[9,768]{1,0:T(8,128)(2,1)S(1)}, u32[]{:S(2)}, u32[]{:S(2)}) %collective-permute-start.18) | collective-permute-done | bytes 13856 | tf_op jit(solution)/shard_map/ppermute | solution.py:117
  71.7 0.1 broadcast_select_fusion.9
  71.9 1.2 %collective-permute-done.19 = bf16[36,576]{1,0:T(8,128)(2,1)S(1)} collective-permute-done((bf16[36,576]{1,0:T(8,128)(2,1)S(1)}, bf16[36,576]{1,0:T(8,128)(2,1)S(1)}, u32[]{:S(2)}, u32[]{:S(2)}) %collective-permute-start.19) | collective-permute-done | bytes 41504 | tf_op jit(solution)/shard_map/ppermute | solution.py:117
  73.1 0.9 %fusion = f32[192,384]{1,0:T(8,128)} fusion(bf16[36,384]{1,0:T(8,128)(2,1)S(1)} %slice.132, bf16[36,384]{1,0:T(8,128)(2,1)S(1)} %slice.130, bf16[36,192]{1,0:T(8,128)(2,1)S(1)} %slice.131, bf16[36,192]{1,0:T(8,128)(2,1)S(1)} %get-tuple-element.53), kind=kOutput, calls=%fused_computation.8 | convolution fusion | flops 10930176 | bytes 377856 | tf_op jit(solution)/shard_map/dot_general | solution.py:210
  (47 shorter events, 0.8 us)
Async XLA Ops:
  1.1 14.1 %collective-permute-start.1 = (bf16[1,8,128,128]{3,2,1,0:T(8,128)(2,1)S(1)}, bf16[1,8,128,128]{3,2,1,0:T(8,128)(2,1)}, u32[]{:S(2)}, u32[]{:S(2)}) collective-permute-start(bf16[1,8,128,128]{3,2,1,0:T(8,128)(2,1)S(1)} %get-tuple-element.49), channel_id=1, source_target_pairs={{0,16},{4,20},{8,24},{12,28},{16,0},{20,4},{24,8},{28,12},{1,17},{... | collective-permute-start | bytes 786440 | tf_op jit(solution)/shard_map/ppermute | solution.py:117
  4.1 11.1 %collective-permute-start = (bf16[1,8,128,128]{3,2,1,0:T(8,128)(2,1)S(1)}, bf16[1,8,128,128]{3,2,1,0:T(8,128)(2,1)}, u32[]{:S(2)}, u32[]{:S(2)}) collective-permute-start(bf16[1,8,128,128]{3,2,1,0:T(8,128)(2,1)S(1)} %get-tuple-element.50), channel_id=1, source_target_pairs={{0,8},{4,12},{8,0},{12,4},{16,24},{20,28},{24,16},{28,20},{1,9},{5... | collective-permute-start | bytes 786440 | tf_op jit(solution)/shard_map/ppermute | solution.py:117
  7.5 2.2 %copy-start.2 = (s32[3]{0:T(128)S(1)}, s32[3]{0:T(128)}, u32[]{:S(2)}) copy-start(s32[3]{0:T(128)} %param.11) | copy-start | bytes 40
  7.5 2.2 %copy-start.4 = (f32[8]{0:T(128)S(1)}, f32[8]{0:T(128)}, u32[]{:S(2)}) copy-start(f32[8]{0:T(128)} %param.8) | copy-start | bytes 100
  7.5 2.4 %copy-start.1 = (s32[3,1536]{1,0:T(4,128)S(1)}, s32[3,1536]{1,0:T(4,128)}, u32[]{:S(2)}) copy-start(s32[3,1536]{1,0:T(4,128)} %param.10) | copy-start | bytes 55300
  7.5 2.4 %copy-start.3 = (f32[3]{0:T(128)S(1)}, f32[3]{0:T(128)}, u32[]{:S(2)}) copy-start(f32[3]{0:T(128)} %param.9) | copy-start | bytes 40
  7.5 5.9 %collective-permute-start.2 = (bf16[1,16,128,128]{3,2,1,0:T(8,128)(2,1)}, bf16[1,16,128,128]{3,2,1,0:T(8,128)(2,1)S(1)}, u32[]{:S(2)}, u32[]{:S(2)}) collective-permute-start(bf16[1,16,128,128]{3,2,1,0:T(8,128)(2,1)} %constant_dynamic-slice_fusion.6), channel_id=1, source_target_pairs={{0,4},{4,0},{8,12},{12,8},{16,20},{20,16},{24,28},{28,24},{1,5},{5... | collective-permute-start | bytes 1572872 | tf_op jit(solution)/shard_map/ppermute | solution.py:117
  9.1 13.9 %collective-permute-start.5 = (bf16[3,16,128,128]{3,2,1,0:T(8,128)(2,1)S(1)}, bf16[3,16,128,128]{3,2,1,0:T(8,128)(2,1)}, u32[]{:S(2)}, u32[]{:S(2)}) collective-permute-start(bf16[3,16,128,128]{3,2,1,0:T(8,128)(2,1)S(1)} %constant_dynamic-slice_fusion.5), channel_id=1, source_target_pairs={{0,4},{4,0},{8,12},{12,8},{16,20},{20,16},{24,28},{28,24},{1,5},{5... | collective-permute-start | bytes 4718600 | tf_op jit(solution)/shard_map/ppermute | solution.py:117
  14.2 8.6 %collective-permute-start.4 = (bf16[1,8,128,128]{3,2,1,0:T(8,128)(2,1)}, bf16[1,8,128,128]{3,2,1,0:T(8,128)(2,1)}, u32[]{:S(2)}, u32[]{:S(2)}) collective-permute-start(bf16[1,8,128,128]{3,2,1,0:T(8,128)(2,1)} %get-tuple-element.51), channel_id=1, source_target_pairs={{0,16},{4,20},{8,24},{12,28},{16,0},{20,4},{24,8},{28,12},{1,17},{... | collective-permute-start | bytes 786440 | tf_op jit(solution)/shard_map/ppermute | solution.py:117
  14.7 8.3 %collective-permute-start.3 = (bf16[1,8,128,128]{3,2,1,0:T(8,128)(2,1)}, bf16[1,8,128,128]{3,2,1,0:T(8,128)(2,1)}, u32[]{:S(2)}, u32[]{:S(2)}) collective-permute-start(bf16[1,8,128,128]{3,2,1,0:T(8,128)(2,1)} %get-tuple-element.52), channel_id=1, source_target_pairs={{0,8},{4,12},{8,0},{12,4},{16,24},{20,28},{24,16},{28,20},{1,9},{5... | collective-permute-start | bytes 786440 | tf_op jit(solution)/shard_map/ppermute | solution.py:117
  23.0 8.0 %copy-start = (bf16[3,32,128,128]{3,2,1,0:T(8,128)(2,1)S(1)}, bf16[3,32,128,128]{3,2,1,0:T(8,128)(2,1)}, u32[]{:S(2)}) copy-start(bf16[3,32,128,128]{3,2,1,0:T(8,128)(2,1)} %param.7) | copy-start | bytes 9437188
  25.4 9.3 %collective-permute-start.6 = (bf16[8,128,128]{2,1,0:T(8,128)(2,1)S(1)}, bf16[8,128,128]{2,1,0:T(8,128)(2,1)S(1)}, u32[]{:S(2)}, u32[]{:S(2)}) collective-permute-start(bf16[8,128,128]{2,1,0:T(8,128)(2,1)S(1)} %get-tuple-element.25), channel_id=1, source_target_pairs={{0,16},{4,20},{8,24},{12,28},{16,0},{20,4},{24,8},{28,12},{1,17},{... | collective-permute-start | bytes 786440 | tf_op jit(solution)/shard_map/ppermute | solution.py:117
  27.0 9.2 %collective-permute-start.7 = (bf16[8,128,128]{2,1,0:T(8,128)(2,1)S(1)}, bf16[8,128,128]{2,1,0:T(8,128)(2,1)S(1)}, u32[]{:S(2)}, u32[]{:S(2)}) collective-permute-start(bf16[8,128,128]{2,1,0:T(8,128)(2,1)S(1)} %get-tuple-element.26), channel_id=1, source_target_pairs={{0,8},{4,12},{8,0},{12,4},{16,24},{20,28},{24,16},{28,20},{1,9},{5... | collective-permute-start | bytes 786440 | tf_op jit(solution)/shard_map/ppermute | solution.py:117
  27.6 14.6 %collective-permute-start.8 = (bf16[8,128,128]{2,1,0:T(8,128)(2,1)S(1)}, bf16[8,128,128]{2,1,0:T(8,128)(2,1)S(1)}, u32[]{:S(2)}, u32[]{:S(2)}) collective-permute-start(bf16[8,128,128]{2,1,0:T(8,128)(2,1)S(1)} %get-tuple-element.30), channel_id=1, source_target_pairs={{0,16},{4,20},{8,24},{12,28},{16,0},{20,4},{24,8},{28,12},{1,17},{... | collective-permute-start | bytes 786440 | tf_op jit(solution)/shard_map/ppermute | solution.py:117
  27.9 14.3 %collective-permute-start.9 = (bf16[8,128,128]{2,1,0:T(8,128)(2,1)S(1)}, bf16[8,128,128]{2,1,0:T(8,128)(2,1)S(1)}, u32[]{:S(2)}, u32[]{:S(2)}) collective-permute-start(bf16[8,128,128]{2,1,0:T(8,128)(2,1)S(1)} %get-tuple-element.31), channel_id=1, source_target_pairs={{0,8},{4,12},{8,0},{12,4},{16,24},{20,28},{24,16},{28,20},{1,9},{5... | collective-permute-start | bytes 786440 | tf_op jit(solution)/shard_map/ppermute | solution.py:117
  29.6 18.3 %collective-permute-start.10 = (bf16[8,128,128]{2,1,0:T(8,128)(2,1)S(1)}, bf16[8,128,128]{2,1,0:T(8,128)(2,1)S(1)}, u32[]{:S(2)}, u32[]{:S(2)}) collective-permute-start(bf16[8,128,128]{2,1,0:T(8,128)(2,1)S(1)} %get-tuple-element.32), channel_id=1, source_target_pairs={{0,16},{4,20},{8,24},{12,28},{16,0},{20,4},{24,8},{28,12},{1,17},{... | collective-permute-start | bytes 786440 | tf_op jit(solution)/shard_map/ppermute | solution.py:117
  34.8 13.1 %collective-permute-start.11 = (bf16[8,128,128]{2,1,0:T(8,128)(2,1)S(1)}, bf16[8,128,128]{2,1,0:T(8,128)(2,1)S(1)}, u32[]{:S(2)}, u32[]{:S(2)}) collective-permute-start(bf16[8,128,128]{2,1,0:T(8,128)(2,1)S(1)} %get-tuple-element.33), channel_id=1, source_target_pairs={{0,8},{4,12},{8,0},{12,4},{16,24},{20,28},{24,16},{28,20},{1,9},{5... | collective-permute-start | bytes 786440 | tf_op jit(solution)/shard_map/ppermute | solution.py:117
  53.7 1.4 %collective-permute-start.12 = (f32[9,1536]{1,0:T(8,128)S(1)}, f32[9,1536]{1,0:T(8,128)S(1)}, u32[]{:S(2)}, u32[]{:S(2)}) collective-permute-start(f32[9,1536]{1,0:T(8,128)S(1)} %fusion.10), channel_id=1, source_target_pairs={{0,4},{4,0},{8,12},{12,8},{16,20},{20,16},{24,28},{28,24},{1,5},{5... | collective-permute-start | bytes 165896 | tf_op jit(solution)/shard_map/ppermute | solution.py:117
  55.1 5.8 %collective-permute-start.15 = (bf16[9,1536]{1,0:T(8,128)(2,1)S(1)}, bf16[9,1536]{1,0:T(8,128)(2,1)S(1)}, u32[]{:S(2)}, u32[]{:S(2)}) collective-permute-start(bf16[9,1536]{1,0:T(8,128)(2,1)S(1)} %fusion.27), channel_id=1, source_target_pairs={{0,3},{1,0},{2,1},{3,2},{4,7},{5,4},{6,5},{7,6},{8,11},{9,8},{10,9... | collective-permute-start | bytes 82952 | tf_op jit(solution)/shard_map/ppermute | solution.py:188
  58.8 5.3 %collective-permute-start.14 = (bf16[9,1536]{1,0:T(8,128)(2,1)S(1)}, bf16[9,1536]{1,0:T(8,128)(2,1)S(1)}, u32[]{:S(2)}, u32[]{:S(2)}) collective-permute-start(bf16[9,1536]{1,0:T(8,128)(2,1)S(1)} %fusion.27), channel_id=1, source_target_pairs={{0,2},{1,3},{2,0},{3,1},{4,6},{5,7},{6,4},{7,5},{8,10},{9,11},{10,... | collective-permute-start | bytes 82952 | tf_op jit(solution)/shard_map/ppermute | solution.py:188
  58.8 5.9 %collective-permute-start.13 = (bf16[9,1536]{1,0:T(8,128)(2,1)S(1)}, bf16[9,1536]{1,0:T(8,128)(2,1)S(1)}, u32[]{:S(2)}, u32[]{:S(2)}) collective-permute-start(bf16[9,1536]{1,0:T(8,128)(2,1)S(1)} %fusion.27), channel_id=1, source_target_pairs={{0,1},{1,2},{2,3},{3,0},{4,5},{5,6},{6,7},{7,4},{8,9},{9,10},{10,1... | collective-permute-start | bytes 82952 | tf_op jit(solution)/shard_map/ppermute | solution.py:188
  64.8 3.9 %collective-permute-start.16 = (bf16[9,768]{1,0:T(8,128)(2,1)S(1)}, bf16[9,768]{1,0:T(8,128)(2,1)S(1)}, u32[]{:S(2)}, u32[]{:S(2)}) collective-permute-start(bf16[9,768]{1,0:T(8,128)(2,1)S(1)} %get-tuple-element.65), channel_id=1, source_target_pairs={{0,8},{4,12},{8,0},{12,4},{16,24},{20,28},{24,16},{28,20},{1,9},{5... | collective-permute-start | bytes 41480 | tf_op jit(solution)/shard_map/ppermute | solution.py:117
  65.5 3.8 %collective-permute-start.17 = (bf16[9,768]{1,0:T(8,128)(2,1)S(1)}, bf16[9,768]{1,0:T(8,128)(2,1)S(1)}, u32[]{:S(2)}, u32[]{:S(2)}) collective-permute-start(bf16[9,768]{1,0:T(8,128)(2,1)S(1)} %get-tuple-element.66), channel_id=1, source_target_pairs={{0,16},{4,20},{8,24},{12,28},{16,0},{20,4},{24,8},{28,12},{1,17},{... | collective-permute-start | bytes 41480 | tf_op jit(solution)/shard_map/ppermute | solution.py:117
  66.9 4.7 %collective-permute-start.18 = (bf16[9,768]{1,0:T(8,128)(2,1)S(1)}, bf16[9,768]{1,0:T(8,128)(2,1)S(1)}, u32[]{:S(2)}, u32[]{:S(2)}) collective-permute-start(bf16[9,768]{1,0:T(8,128)(2,1)S(1)} %get-tuple-element.67), channel_id=1, source_target_pairs={{0,24},{4,28},{8,16},{12,20},{16,8},{20,12},{24,0},{28,4},{1,25},{... | collective-permute-start | bytes 41480 | tf_op jit(solution)/shard_map/ppermute | solution.py:117
  71.8 1.3 %collective-permute-start.19 = (bf16[36,576]{1,0:T(8,128)(2,1)S(1)}, bf16[36,576]{1,0:T(8,128)(2,1)S(1)}, u32[]{:S(2)}, u32[]{:S(2)}) collective-permute-start(bf16[36,576]{1,0:T(8,128)(2,1)S(1)} %pad_maximum_fusion.3), channel_id=1, source_target_pairs={{0,4},{4,0},{8,12},{12,8},{16,20},{20,16},{24,28},{28,24},{1,5},{5... | collective-permute-start | bytes 124424 | tf_op jit(solution)/shard_map/ppermute | solution.py:117

commit v3 on v2

--- a/solution.py
+++ b/solution.py
@@ -93,7 +93,7 @@
             pltpu.VMEM((length * length, lanes), jnp.float32),
             pltpu.VMEM((keep, lanes), jnp.float32),
         ],
-        compiler_params=pltpu.CompilerParams(vmem_limit_bytes=32 * 2**20),
+        compiler_params=pltpu.CompilerParams(vmem_limit_bytes=24 * 2**20),
         cost_estimate=pl.CostEstimate(flops=4 * 10**9, bytes_accessed=12 * 2**20, transcendentals=0),
         name="round_coeffs",
     )(index, va, vb, c0, c1, table, tx)
@@ -119,8 +119,17 @@
     def half_of(value, which):
         return lax.dynamic_slice_in_dim(value, which * x_half, x_half, 1)
 
-    v_mine = half_of(valence, side)
-    v_swapped = swap(half_of(valence, 1 - side), 1)
+    cut = x_half // 2
+    part_starts = (0, cut)
+
+    def parts_of(which):
+        return [lax.dynamic_slice_in_dim(valence, which * x_half + start, cut, 1) for start in part_starts]
+
+    v_swapped = [swap(part, 1) for part in parts_of(1 - side)]
+    v_mine = parts_of(side)
+    v_swapped, conduction, kept, plan, energy_val = lax.optimization_barrier(
+        (v_swapped, conduction, kept, plan, energy_val)
+    )
     c_mine = half_of(conduction, side)
     c_swapped = swap(half_of(conduction, 1 - side), 1)
 
@@ -151,8 +160,7 @@
     def nearer(r, bit, near, far):
         return jnp.where((relative[r] >> bit) & 1 == 0, near, far)
 
-    cut = x_half // 2
-    parts = [(v_mine[:, :cut], v_swapped[:, :cut]), (v_mine[:, cut:], v_swapped[:, cut:])]
+    parts = list(zip(v_mine, v_swapped))
     orders = [list(range(bits)), list(range(bits))[::-1]]
     if 2 * held <= rounds and bits:
         far_mine = [swap(part[0], 2 << order[0]) for part, order in zip(parts, orders)]

time: 74.3 us -> 68.9 us (0.927)
  waiting for transfers between devices: 21.8 us -> 19.2 us
  local copies, waits for them, and re-layouts: 5.52 us -> 3.02 us
  other arithmetic: 8.49 us -> 7.62 us
    ppermute x17 -> x18, waiting for transfers between devices: 16.9 us -> 14.4 us  [swap(): return lax.ppermute(value, 'band', [(i, i ^ mask) for i in range(n_band)])]
    slice x2 -> x0, local copies, waits for them, and re-layouts: 1.9 us -> none  [the longest x1 1.06 us: per_device(): v_mine[:, cut:]]
    dynamic_slice x2 -> x1, local copies, waits for them, and re-layouts: 3.4 us -> 1.51 us  [half_of(): return lax.dynamic_slice_in_dim(value, which * x_half, x_half, 1)]
    dynamic_slice x0 -> x1, local copies, waits for them, and re-layouts: none -> 1.3 us  [parts_of(): lax.dynamic_slice_in_dim(valence, which * x_half + start, cut, 1)]
    select_n x8 -> x7, other arithmetic: 2.59 us -> 1.72 us  [nearer(): return jnp.where(relative[r] >> bit & 1 == 0, near, far)]
    ppermute x17 -> x18, starting transfers between devices: 15.4 us -> 15.9 us  [swap(): return lax.ppermute(value, 'band', [(i, i ^ mask) for i in range(n_band)])]
  transfers between devices with their start and end apart: 20 -> 21, of which waited for: 12 -> 11; matrix products, arithmetic and copies ran while one was open for 14% -> 11% of each run, Pallas kernels for 15% -> 17%
where the time goes in v3:
time: 68.9 us; the launch traced here: 68.7 us
  starting transfers between devices  20.6 us (30%)
  waiting for transfers between devices  19.2 us (28%)
  Pallas kernels  17 us (25%)
  other arithmetic  7.62 us (11%)
  local copies, waits for them, and re-layouts  3.02 us (4%)
  matrix products  0.95 us (1%)
    pallas_call x3, Pallas kernels, round_coeffs(): pl.pallas_call(round_kernel, out_shape=jax.ShapeDtypeStruct((rows, keep),...  17 us
    ppermute x18, starting transfers between devices, swap(): return lax.ppermute(value, 'band', [(i, i ^ mask) for i in range(n_band)])  15.9 us
    ppermute x18, waiting for transfers between devices, swap(): return lax.ppermute(value, 'band', [(i, i ^ mask) for i in range(n_band)])  14.4 us
    ppermute x3, waiting for transfers between devices, per_device(): lax.ppermute(sent, 'col', [(i, (i + shift) % n_col) for i in range(n_col)])  4.83 us
    ppermute x3, starting transfers between devices, per_device(): lax.ppermute(sent, 'col', [(i, (i + shift) % n_col) for i in range(n_col)])  4.71 us
    mul x1, other arithmetic, per_device(): cas_of(kept[0][:, None] * x_global[None, :] % length, length)  3.17 us
    select_n x7, other arithmetic, nearer(): return jnp.where(relative[r] >> bit & 1 == 0, near, far)  1.72 us
    select_n x1, other arithmetic, per_device(): c1 = jnp.where(side == 0, c_swapped, c_mine)  1.61 us
  transfers between devices with their start and end apart: 21, of which 11 were waited for; matrix products, arithmetic and copies ran while one was open for 11% of the time, Pallas kernels for 17%

profile of v3, /device:TPU:0, one launch (start us, length us, event | category | flops | bytes accessed | tf_op | source)
XLA Modules:
  0.0 68.7 jit_solution(11990471476886424924)
XLA Ops:
  0.0 1.3 %constant_dynamic-slice_fusion.5 = (bf16[1,8,128,128]{3,2,1,0:T(8,128)(2,1)S(1)}, bf16[1,8,128,128]{3,2,1,0:T(8,128)(2,1)S(1)}, bf16[1,8,128,128]{3,2,1,0:T(8,128)(2,1)S(1)}, bf16[1,8,128,128]{3,2,1,0:T(8,128)(2,1)S(1)}) fusion(bf16[1,32,128,128]{3,2,1,0:T(8,128)(2,1)} %param.6, s32[]{:T(128)S(6)} %select_n.213, s32[]{:T(128)S(6)} %select_n.211, ...), kind=kLoop, calls=%fused_computation.79 | loop fusion | bytes 2097168 | tf_op jit(solution)/shard_map/dynamic_slice | solution.py:126
  1.3 0.5 collective-permute-start.3
  1.9 0.1 collective-permute-start.2
  1.9 2.9 %collective-permute-start.1 = (bf16[1,8,128,128]{3,2,1,0:T(8,128)(2,1)S(1)}, bf16[1,8,128,128]{3,2,1,0:T(8,128)(2,1)}, u32[]{:S(2)}, u32[]{:S(2)}) collective-permute-start(bf16[1,8,128,128]{3,2,1,0:T(8,128)(2,1)S(1)} %get-tuple-element.62), channel_id=1, source_target_pairs={{0,16},{4,20},{8,24},{12,28},{16,0},{20,4},{24,8},{28,12},{1,17},{... | collective-permute-start | bytes 786440 | tf_op jit(solution)/shard_map/ppermute | solution.py:117
  4.9 1.5 %collective-permute-start = (bf16[1,8,128,128]{3,2,1,0:T(8,128)(2,1)S(1)}, bf16[1,8,128,128]{3,2,1,0:T(8,128)(2,1)}, u32[]{:S(2)}, u32[]{:S(2)}) collective-permute-start(bf16[1,8,128,128]{3,2,1,0:T(8,128)(2,1)S(1)} %get-tuple-element.63), channel_id=1, source_target_pairs={{0,8},{4,12},{8,0},{12,4},{16,24},{20,28},{24,16},{28,20},{1,9},{5... | collective-permute-start | bytes 786440 | tf_op jit(solution)/shard_map/ppermute | solution.py:117
  6.4 0.3 add_convert_fusion.table_ref
  6.7 0.2 select_reduce_fusion
  7.0 0.6 collective-permute-start.4
  7.6 0.5 collective-permute-start.5
  8.1 1.5 %constant_dynamic-slice_fusion.4 = bf16[3,16,128,128]{3,2,1,0:T(8,128)(2,1)S(1)} fusion(bf16[3,32,128,128]{3,2,1,0:T(8,128)(2,1)} %param.7, s32[]{:T(128)S(6)} %select_n.212), kind=kLoop, calls=%fused_computation.78 | loop fusion | bytes 3145732 | tf_op jit(solution)/shard_map/dynamic_slice | solution.py:120
  9.6 0.1 collective-permute-start.6
  9.7 0.1 subtract_divide_fusion
  9.8 0.1 fusion.24
  9.9 3.2 %add_multiply_fusion.tx_ref = f32[1536,128]{1,0:T(8,128)S(1)} fusion(s32[128]{0:T(128)S(1)} %fusion.25, s32[1536]{0:T(1024)S(1)} %get-tuple-element.48), kind=kLoop, calls=%fused_computation.12 | loop fusion | flops 3145728 | bytes 793088 | tf_op jit(solution)/shard_map/mul | solution.py:141
  13.1 0.1 fusion.23
  13.2 0.1 div.35
  13.3 0.9 %collective-permute-done = bf16[1,8,128,128]{3,2,1,0:T(8,128)(2,1)} collective-permute-done((bf16[1,8,128,128]{3,2,1,0:T(8,128)(2,1)S(1)}, bf16[1,8,128,128]{3,2,1,0:T(8,128)(2,1)}, u32[]{:S(2)}, u32[]{:S(2)}) %collective-permute-start) | collective-permute-done | bytes 262176 | tf_op jit(solution)/shard_map/ppermute | solution.py:117
  14.2 4.4 %collective-permute-done.4 = bf16[1,8,128,128]{3,2,1,0:T(8,128)(2,1)} collective-permute-done((bf16[1,8,128,128]{3,2,1,0:T(8,128)(2,1)S(1)}, bf16[1,8,128,128]{3,2,1,0:T(8,128)(2,1)}, u32[]{:S(2)}, u32[]{:S(2)}) %collective-permute-start.4) | collective-permute-done | bytes 262176 | tf_op jit(solution)/shard_map/ppermute | solution.py:117
  18.6 1.5 %fusion.9 = (bf16[8,128,128]{2,1,0:T(8,128)(2,1)S(1)}, bf16[8,128,128]{2,1,0:T(8,128)(2,1)S(1)}, bf16[8,128,128]{2,1,0:T(8,128)(2,1)S(1)}, bf16[8,128,128]{2,1,0...) fusion(bf16[1,8,128,128]{3,2,1,0:T(8,128)(2,1)} %collective-permute-done.4, ...), kind=kLoop, calls=%fused_computation.27 | loop fusion | flops 2359296 | bytes 3671168 | tf_op jit(solution)/shard_map/jit(_where)/select_n | solution.py:161
  20.1 0.3 collective-permute-start.7
  20.5 1.7 %collective-permute-start.8 = (bf16[8,128,128]{2,1,0:T(8,128)(2,1)S(1)}, bf16[8,128,128]{2,1,0:T(8,128)(2,1)S(1)}, u32[]{:S(2)}, u32[]{:S(2)}) collective-permute-start(bf16[8,128,128]{2,1,0:T(8,128)(2,1)S(1)} %get-tuple-element.38), channel_id=1, source_target_pairs={{0,8},{4,12},{8,0},{12,4},{16,24},{20,28},{24,16},{28,20},{1,9},{5... | collective-permute-start | bytes 786440 | tf_op jit(solution)/shard_map/ppermute | solution.py:117
  22.2 1.5 %collective-permute-start.9 = (bf16[8,128,128]{2,1,0:T(8,128)(2,1)S(1)}, bf16[8,128,128]{2,1,0:T(8,128)(2,1)S(1)}, u32[]{:S(2)}, u32[]{:S(2)}) collective-permute-start(bf16[8,128,128]{2,1,0:T(8,128)(2,1)S(1)} %get-tuple-element.42), channel_id=1, source_target_pairs={{0,16},{4,20},{8,24},{12,28},{16,0},{20,4},{24,8},{28,12},{1,17},{... | collective-permute-start | bytes 786440 | tf_op jit(solution)/shard_map/ppermute | solution.py:117
  23.7 0.5 collective-permute-start.10
  24.3 0.3 collective-permute-start.11
  24.6 1.6 %broadcast_select_fusion = (bf16[3,16,128,128]{3,2,1,0:T(8,128)(2,1)S(1)}, bf16[3,16,128,128]{3,2,1,0:T(8,128)(2,1)S(1)}) fusion(bf16[3,16,128,128]{3,2,1,0:T(8,128)(2,1)} %collective-permute-done.6, pred[]{:T(512)S(6)} %eq.117, bf16[3,32,128,128]{3,2,1,0:T(8,128)(2,1)S(1)} %copy-done, s32[]{:T(128)S(6)} %select_n.210), kind=kLoop, calls=%fused_computation | loop fusion | flops 1572864 | bytes 6291461 | tf_op jit(solution)/shard_map/jit(_where)/select_n | solution.py:186
  26.2 3.3 %collective-permute-done.7 = bf16[8,128,128]{2,1,0:T(8,128)(2,1)S(1)} collective-permute-done((bf16[8,128,128]{2,1,0:T(8,128)(2,1)S(1)}, bf16[8,128,128]{2,1,0:T(8,128)(2,1)S(1)}, u32[]{:S(2)}, u32[]{:S(2)}) %collective-permute-start.7) | collective-permute-done | bytes 262176 | tf_op jit(solution)/shard_map/ppermute | solution.py:117
  29.5 1.5 %collective-permute-start.12 = (bf16[8,128,128]{2,1,0:T(8,128)(2,1)S(1)}, bf16[8,128,128]{2,1,0:T(8,128)(2,1)S(1)}, u32[]{:S(2)}, u32[]{:S(2)}) collective-permute-start(bf16[8,128,128]{2,1,0:T(8,128)(2,1)S(1)} %get-tuple-element.45), channel_id=1, source_target_pairs={{0,8},{4,12},{8,0},{12,4},{16,24},{20,28},{24,16},{28,20},{1,9},{5... | collective-permute-start | bytes 786440 | tf_op jit(solution)/shard_map/ppermute | solution.py:117
  31.0 5.8 %round_coeffs.3 = f32[8,1536]{1,0:T(8,128)S(1)} custom-call(s32[1536]{0:T(1024)S(1)} %get-tuple-element.32.index_ref, bf16[8,128,128]{2,1,0:T(8,128)(2,1)S(1)} %broadcast_select_fusion.7.va_ref, bf16[8,128,128]{2,1,0:T(8,128)(2,1)S(1)} %broadcast_select_fusion.6.vb_ref, bf16[3,16,128,128]{3,2,1,0:T(8,128)(2,1)S(1)} %get-tuple-element.54.c0_ref, ...), custom_call_target="tpu_custom_call" | custom-call | flops 4000000000 | bytes 12582912 | tf_op jit(solution)/shard_map/round_coeffs/pallas_call | solution.py:86
  37.0 5.6 %round_coeffs.4 = f32[8,1536]{1,0:T(8,128)S(1)} custom-call(s32[1536]{0:T(1024)S(1)} %get-tuple-element.32.index_ref, bf16[8,128,128]{2,1,0:T(8,128)(2,1)S(1)} %broadcast_select_fusion.4.va_ref, bf16[8,128,128]{2,1,0:T(8,128)(2,1)S(1)} %broadcast_select_fusion.5.vb_ref, bf16[3,16,128,128]{3,2,1,0:T(8,128)(2,1)S(1)} %get-tuple-element.54.c0_ref, ...), custom_call_target="tpu_custom_call" | custom-call | flops 4000000000 | bytes 12582912 | tf_op jit(solution)/shard_map/round_coeffs/pallas_call | solution.py:86
  42.7 5.6 %round_coeffs.5 = f32[8,1536]{1,0:T(8,128)S(1)} custom-call(s32[1536]{0:T(1024)S(1)} %get-tuple-element.32.index_ref, bf16[8,128,128]{2,1,0:T(8,128)(2,1)S(1)} %broadcast_select_fusion.2.va_ref, bf16[8,128,128]{2,1,0:T(8,128)(2,1)S(1)} %broadcast_select_fusion.3.vb_ref, bf16[3,16,128,128]{3,2,1,0:T(8,128)(2,1)S(1)} %get-tuple-element.54.c0_ref, ...), custom_call_target="tpu_custom_call" | custom-call | flops 4000000000 | bytes 12582912 | tf_op jit(solution)/shard_map/round_coeffs/pallas_call | solution.py:86
  48.4 0.1 collective-permute-start.13
  48.5 1.3 %collective-permute-done.13 = f32[9,1536]{1,0:T(8,128)S(1)} collective-permute-done((f32[9,1536]{1,0:T(8,128)S(1)}, f32[9,1536]{1,0:T(8,128)S(1)}, u32[]{:S(2)}, u32[]{:S(2)}) %collective-permute-start.13) | collective-permute-done | bytes 55328 | tf_op jit(solution)/shard_map/ppermute | solution.py:117
  49.8 3.7 %collective-permute-start.16 = (bf16[9,1536]{1,0:T(8,128)(2,1)S(1)}, bf16[9,1536]{1,0:T(8,128)(2,1)S(1)}, u32[]{:S(2)}, u32[]{:S(2)}) collective-permute-start(bf16[9,1536]{1,0:T(8,128)(2,1)S(1)} %fusion.27), channel_id=1, source_target_pairs={{0,3},{1,0},{2,1},{3,2},{4,7},{5,4},{6,5},{7,6},{8,11},{9,8},{10,9... | collective-permute-start | bytes 82952 | tf_op jit(solution)/shard_map/ppermute | solution.py:196
  53.5 1.1 %collective-permute-start.14 = (bf16[9,1536]{1,0:T(8,128)(2,1)S(1)}, bf16[9,1536]{1,0:T(8,128)(2,1)S(1)}, u32[]{:S(2)}, u32[]{:S(2)}) collective-permute-start(bf16[9,1536]{1,0:T(8,128)(2,1)S(1)} %fusion.27), channel_id=1, source_target_pairs={{0,1},{1,2},{2,3},{3,0},{4,5},{5,6},{6,7},{7,4},{8,9},{9,10},{10,1... | collective-permute-start | bytes 82952 | tf_op jit(solution)/shard_map/ppermute | solution.py:196
  54.6 1.0 %collective-permute-done.16 = bf16[9,1536]{1,0:T(8,128)(2,1)S(1)} collective-permute-done((bf16[9,1536]{1,0:T(8,128)(2,1)S(1)}, bf16[9,1536]{1,0:T(8,128)(2,1)S(1)}, u32[]{:S(2)}, u32[]{:S(2)}) %collective-permute-start.16) | collective-permute-done | bytes 27680 | tf_op jit(solution)/shard_map/ppermute | solution.py:196
  55.6 3.2 %collective-permute-done.15 = bf16[9,1536]{1,0:T(8,128)(2,1)S(1)} collective-permute-done((bf16[9,1536]{1,0:T(8,128)(2,1)S(1)}, bf16[9,1536]{1,0:T(8,128)(2,1)S(1)}, u32[]{:S(2)}, u32[]{:S(2)}) %collective-permute-start.15) | collective-permute-done | bytes 27680 | tf_op jit(solution)/shard_map/ppermute | solution.py:196
  58.8 0.6 collective-permute-done.14
  59.4 0.1 multiply_convert_fusion
  59.5 0.6 collective-permute-start.17
  60.2 1.4 %collective-permute-start.18 = (bf16[9,768]{1,0:T(8,128)(2,1)S(1)}, bf16[9,768]{1,0:T(8,128)(2,1)S(1)}, u32[]{:S(2)}, u32[]{:S(2)}) collective-permute-start(bf16[9,768]{1,0:T(8,128)(2,1)S(1)} %get-tuple-element.78), channel_id=1, source_target_pairs={{0,16},{4,20},{8,24},{12,28},{16,0},{20,4},{24,8},{28,12},{1,17},{... | collective-permute-start | bytes 41480 | tf_op jit(solution)/shard_map/ppermute | solution.py:117
  61.6 1.5 %collective-permute-start.19 = (bf16[9,768]{1,0:T(8,128)(2,1)S(1)}, bf16[9,768]{1,0:T(8,128)(2,1)S(1)}, u32[]{:S(2)}, u32[]{:S(2)}) collective-permute-start(bf16[9,768]{1,0:T(8,128)(2,1)S(1)} %get-tuple-element.79), channel_id=1, source_target_pairs={{0,24},{4,28},{8,16},{12,20},{16,8},{20,12},{24,0},{28,4},{1,25},{... | collective-permute-start | bytes 41480 | tf_op jit(solution)/shard_map/ppermute | solution.py:117
  63.1 0.3 collective-permute-done.17
  63.4 0.6 collective-permute-done.18
  64.0 2.3 %collective-permute-done.19 = bf16[9,768]{1,0:T(8,128)(2,1)S(1)} collective-permute-done((bf16[9,768]{1,0:T(8,128)(2,1)S(1)}, bf16[9,768]{1,0:T(8,128)(2,1)S(1)}, u32[]{:S(2)}, u32[]{:S(2)}) %collective-permute-start.19) | collective-permute-done | bytes 13856 | tf_op jit(solution)/shard_map/ppermute | solution.py:117
  66.4 0.1 broadcast_select_fusion.9
  66.5 0.1 collective-permute-start.20
  66.6 1.2 %collective-permute-done.20 = bf16[36,576]{1,0:T(8,128)(2,1)S(1)} collective-permute-done((bf16[36,576]{1,0:T(8,128)(2,1)S(1)}, bf16[36,576]{1,0:T(8,128)(2,1)S(1)}, u32[]{:S(2)}, u32[]{:S(2)}) %collective-permute-start.20) | collective-permute-done | bytes 41504 | tf_op jit(solution)/shard_map/ppermute | solution.py:117
  67.8 0.9 %fusion = f32[192,384]{1,0:T(8,128)} fusion(bf16[36,384]{1,0:T(8,128)(2,1)S(1)} %slice.114, bf16[36,384]{1,0:T(8,128)(2,1)S(1)} %slice.112, bf16[36,192]{1,0:T(8,128)(2,1)S(1)} %slice.113, bf16[36,192]{1,0:T(8,128)(2,1)S(1)} %get-tuple-element.65), kind=kOutput, calls=%fused_computation.8 | convolution fusion | flops 10930176 | bytes 377856 | tf_op jit(solution)/shard_map/dot_general | solution.py:218
  (46 shorter events, 0.6 us)
Async XLA Ops:
  0.0 6.7 %copy-start.2 = (s32[3]{0:T(128)S(1)}, s32[3]{0:T(128)}, u32[]{:S(2)}) copy-start(s32[3]{0:T(128)} %param.11) | copy-start | bytes 40
  0.0 6.9 %copy-start.1 = (s32[3,1536]{1,0:T(4,128)S(1)}, s32[3,1536]{1,0:T(4,128)}, u32[]{:S(2)}) copy-start(s32[3,1536]{1,0:T(4,128)} %param.10) | copy-start | bytes 55300
  0.0 6.7 %copy-start.4 = (f32[8]{0:T(128)S(1)}, f32[8]{0:T(128)}, u32[]{:S(2)}) copy-start(f32[8]{0:T(128)} %param.8) | copy-start | bytes 100
  1.3 5.4 %collective-permute-start.3 = (bf16[1,8,128,128]{3,2,1,0:T(8,128)(2,1)S(1)}, bf16[1,8,128,128]{3,2,1,0:T(8,128)(2,1)S(1)}, u32[]{:S(2)}, u32[]{:S(2)}) collective-permute-start(bf16[1,8,128,128]{3,2,1,0:T(8,128)(2,1)S(1)} %get-tuple-element.61), channel_id=1, source_target_pairs={{0,4},{4,0},{8,12},{12,8},{16,20},{20,16},{24,28},{28,24},{1,5},{5... | collective-permute-start | bytes 786440 | tf_op jit(solution)/shard_map/ppermute | solution.py:117
  1.9 4.8 %collective-permute-start.2 = (bf16[1,8,128,128]{3,2,1,0:T(8,128)(2,1)S(1)}, bf16[1,8,128,128]{3,2,1,0:T(8,128)(2,1)S(1)}, u32[]{:S(2)}, u32[]{:S(2)}) collective-permute-start(bf16[1,8,128,128]{3,2,1,0:T(8,128)(2,1)S(1)} %get-tuple-element.64), channel_id=1, source_target_pairs={{0,4},{4,0},{8,12},{12,8},{16,20},{20,16},{24,28},{28,24},{1,5},{5... | collective-permute-start | bytes 786440 | tf_op jit(solution)/shard_map/ppermute | solution.py:117
  1.9 11.3 %collective-permute-start.1 = (bf16[1,8,128,128]{3,2,1,0:T(8,128)(2,1)S(1)}, bf16[1,8,128,128]{3,2,1,0:T(8,128)(2,1)}, u32[]{:S(2)}, u32[]{:S(2)}) collective-permute-start(bf16[1,8,128,128]{3,2,1,0:T(8,128)(2,1)S(1)} %get-tuple-element.62), channel_id=1, source_target_pairs={{0,16},{4,20},{8,24},{12,28},{16,0},{20,4},{24,8},{28,12},{1,17},{... | collective-permute-start | bytes 786440 | tf_op jit(solution)/shard_map/ppermute | solution.py:117
  4.9 9.3 %collective-permute-start = (bf16[1,8,128,128]{3,2,1,0:T(8,128)(2,1)S(1)}, bf16[1,8,128,128]{3,2,1,0:T(8,128)(2,1)}, u32[]{:S(2)}, u32[]{:S(2)}) collective-permute-start(bf16[1,8,128,128]{3,2,1,0:T(8,128)(2,1)S(1)} %get-tuple-element.63), channel_id=1, source_target_pairs={{0,8},{4,12},{8,0},{12,4},{16,24},{20,28},{24,16},{28,20},{1,9},{5... | collective-permute-start | bytes 786440 | tf_op jit(solution)/shard_map/ppermute | solution.py:117
  7.0 2.8 %copy-start.3 = (f32[3]{0:T(128)S(1)}, f32[3]{0:T(128)}, u32[]{:S(2)}) copy-start(f32[3]{0:T(128)} %param.9) | copy-start | bytes 40
  7.0 11.6 %collective-permute-start.4 = (bf16[1,8,128,128]{3,2,1,0:T(8,128)(2,1)S(1)}, bf16[1,8,128,128]{3,2,1,0:T(8,128)(2,1)}, u32[]{:S(2)}, u32[]{:S(2)}) collective-permute-start(bf16[1,8,128,128]{3,2,1,0:T(8,128)(2,1)S(1)} %collective-permute-done.2), channel_id=1, source_target_pairs={{0,8},{4,12},{8,0},{12,4},{16,24},{20,28},{24,16},{28,20},{1,9},{5... | collective-permute-start | bytes 786440 | tf_op jit(solution)/shard_map/ppermute | solution.py:117
  7.6 11.0 %collective-permute-start.5 = (bf16[1,8,128,128]{3,2,1,0:T(8,128)(2,1)S(1)}, bf16[1,8,128,128]{3,2,1,0:T(8,128)(2,1)}, u32[]{:S(2)}, u32[]{:S(2)}) collective-permute-start(bf16[1,8,128,128]{3,2,1,0:T(8,128)(2,1)S(1)} %collective-permute-done.3), channel_id=1, source_target_pairs={{0,16},{4,20},{8,24},{12,28},{16,0},{20,4},{24,8},{28,12},{1,17},{... | collective-permute-start | bytes 786440 | tf_op jit(solution)/shard_map/ppermute | solution.py:117
  9.6 9.0 %collective-permute-start.6 = (bf16[3,16,128,128]{3,2,1,0:T(8,128)(2,1)S(1)}, bf16[3,16,128,128]{3,2,1,0:T(8,128)(2,1)}, u32[]{:S(2)}, u32[]{:S(2)}) collective-permute-start(bf16[3,16,128,128]{3,2,1,0:T(8,128)(2,1)S(1)} %constant_dynamic-slice_fusion.4), channel_id=1, source_target_pairs={{0,4},{4,0},{8,12},{12,8},{16,20},{20,16},{24,28},{28,24},{1,5},{5... | collective-permute-start | bytes 4718600 | tf_op jit(solution)/shard_map/ppermute | solution.py:117
  18.6 5.9 %copy-start = (bf16[3,32,128,128]{3,2,1,0:T(8,128)(2,1)S(1)}, bf16[3,32,128,128]{3,2,1,0:T(8,128)(2,1)}, u32[]{:S(2)}) copy-start(bf16[3,32,128,128]{3,2,1,0:T(8,128)(2,1)} %param.7) | copy-start | bytes 9437188
  20.1 9.3 %collective-permute-start.7 = (bf16[8,128,128]{2,1,0:T(8,128)(2,1)S(1)}, bf16[8,128,128]{2,1,0:T(8,128)(2,1)S(1)}, u32[]{:S(2)}, u32[]{:S(2)}) collective-permute-start(bf16[8,128,128]{2,1,0:T(8,128)(2,1)S(1)} %get-tuple-element.37), channel_id=1, source_target_pairs={{0,16},{4,20},{8,24},{12,28},{16,0},{20,4},{24,8},{28,12},{1,17},{... | collective-permute-start | bytes 786440 | tf_op jit(solution)/shard_map/ppermute | solution.py:117
  20.5 10.5 %collective-permute-start.8 = (bf16[8,128,128]{2,1,0:T(8,128)(2,1)S(1)}, bf16[8,128,128]{2,1,0:T(8,128)(2,1)S(1)}, u32[]{:S(2)}, u32[]{:S(2)}) collective-permute-start(bf16[8,128,128]{2,1,0:T(8,128)(2,1)S(1)} %get-tuple-element.38), channel_id=1, source_target_pairs={{0,8},{4,12},{8,0},{12,4},{16,24},{20,28},{24,16},{28,20},{1,9},{5... | collective-permute-start | bytes 786440 | tf_op jit(solution)/shard_map/ppermute | solution.py:117
  22.2 14.6 %collective-permute-start.9 = (bf16[8,128,128]{2,1,0:T(8,128)(2,1)S(1)}, bf16[8,128,128]{2,1,0:T(8,128)(2,1)S(1)}, u32[]{:S(2)}, u32[]{:S(2)}) collective-permute-start(bf16[8,128,128]{2,1,0:T(8,128)(2,1)S(1)} %get-tuple-element.42), channel_id=1, source_target_pairs={{0,16},{4,20},{8,24},{12,28},{16,0},{20,4},{24,8},{28,12},{1,17},{... | collective-permute-start | bytes 786440 | tf_op jit(solution)/shard_map/ppermute | solution.py:117
  23.7 13.2 %collective-permute-start.10 = (bf16[8,128,128]{2,1,0:T(8,128)(2,1)S(1)}, bf16[8,128,128]{2,1,0:T(8,128)(2,1)S(1)}, u32[]{:S(2)}, u32[]{:S(2)}) collective-permute-start(bf16[8,128,128]{2,1,0:T(8,128)(2,1)S(1)} %get-tuple-element.43), channel_id=1, source_target_pairs={{0,8},{4,12},{8,0},{12,4},{16,24},{20,28},{24,16},{28,20},{1,9},{5... | collective-permute-start | bytes 786440 | tf_op jit(solution)/shard_map/ppermute | solution.py:117
  24.3 18.3 %collective-permute-start.11 = (bf16[8,128,128]{2,1,0:T(8,128)(2,1)S(1)}, bf16[8,128,128]{2,1,0:T(8,128)(2,1)S(1)}, u32[]{:S(2)}, u32[]{:S(2)}) collective-permute-start(bf16[8,128,128]{2,1,0:T(8,128)(2,1)S(1)} %get-tuple-element.44), channel_id=1, source_target_pairs={{0,16},{4,20},{8,24},{12,28},{16,0},{20,4},{24,8},{28,12},{1,17},{... | collective-permute-start | bytes 786440 | tf_op jit(solution)/shard_map/ppermute | solution.py:117
  29.5 13.2 %collective-permute-start.12 = (bf16[8,128,128]{2,1,0:T(8,128)(2,1)S(1)}, bf16[8,128,128]{2,1,0:T(8,128)(2,1)S(1)}, u32[]{:S(2)}, u32[]{:S(2)}) collective-permute-start(bf16[8,128,128]{2,1,0:T(8,128)(2,1)S(1)} %get-tuple-element.45), channel_id=1, source_target_pairs={{0,8},{4,12},{8,0},{12,4},{16,24},{20,28},{24,16},{28,20},{1,9},{5... | collective-permute-start | bytes 786440 | tf_op jit(solution)/shard_map/ppermute | solution.py:117
  48.4 1.4 %collective-permute-start.13 = (f32[9,1536]{1,0:T(8,128)S(1)}, f32[9,1536]{1,0:T(8,128)S(1)}, u32[]{:S(2)}, u32[]{:S(2)}) collective-permute-start(f32[9,1536]{1,0:T(8,128)S(1)} %fusion.10), channel_id=1, source_target_pairs={{0,4},{4,0},{8,12},{12,8},{16,20},{20,16},{24,28},{28,24},{1,5},{5... | collective-permute-start | bytes 165896 | tf_op jit(solution)/shard_map/ppermute | solution.py:117
  49.8 5.8 %collective-permute-start.16 = (bf16[9,1536]{1,0:T(8,128)(2,1)S(1)}, bf16[9,1536]{1,0:T(8,128)(2,1)S(1)}, u32[]{:S(2)}, u32[]{:S(2)}) collective-permute-start(bf16[9,1536]{1,0:T(8,128)(2,1)S(1)} %fusion.27), channel_id=1, source_target_pairs={{0,3},{1,0},{2,1},{3,2},{4,7},{5,4},{6,5},{7,6},{8,11},{9,8},{10,9... | collective-permute-start | bytes 82952 | tf_op jit(solution)/shard_map/ppermute | solution.py:196
  53.5 5.3 %collective-permute-start.15 = (bf16[9,1536]{1,0:T(8,128)(2,1)S(1)}, bf16[9,1536]{1,0:T(8,128)(2,1)S(1)}, u32[]{:S(2)}, u32[]{:S(2)}) collective-permute-start(bf16[9,1536]{1,0:T(8,128)(2,1)S(1)} %fusion.27), channel_id=1, source_target_pairs={{0,2},{1,3},{2,0},{3,1},{4,6},{5,7},{6,4},{7,5},{8,10},{9,11},{10,... | collective-permute-start | bytes 82952 | tf_op jit(solution)/shard_map/ppermute | solution.py:196
  53.5 5.9 %collective-permute-start.14 = (bf16[9,1536]{1,0:T(8,128)(2,1)S(1)}, bf16[9,1536]{1,0:T(8,128)(2,1)S(1)}, u32[]{:S(2)}, u32[]{:S(2)}) collective-permute-start(bf16[9,1536]{1,0:T(8,128)(2,1)S(1)} %fusion.27), channel_id=1, source_target_pairs={{0,1},{1,2},{2,3},{3,0},{4,5},{5,6},{6,7},{7,4},{8,9},{9,10},{10,1... | collective-permute-start | bytes 82952 | tf_op jit(solution)/shard_map/ppermute | solution.py:196
  59.5 3.9 %collective-permute-start.17 = (bf16[9,768]{1,0:T(8,128)(2,1)S(1)}, bf16[9,768]{1,0:T(8,128)(2,1)S(1)}, u32[]{:S(2)}, u32[]{:S(2)}) collective-permute-start(bf16[9,768]{1,0:T(8,128)(2,1)S(1)} %get-tuple-element.77), channel_id=1, source_target_pairs={{0,8},{4,12},{8,0},{12,4},{16,24},{20,28},{24,16},{28,20},{1,9},{5... | collective-permute-start | bytes 41480 | tf_op jit(solution)/shard_map/ppermute | solution.py:117
  60.2 3.8 %collective-permute-start.18 = (bf16[9,768]{1,0:T(8,128)(2,1)S(1)}, bf16[9,768]{1,0:T(8,128)(2,1)S(1)}, u32[]{:S(2)}, u32[]{:S(2)}) collective-permute-start(bf16[9,768]{1,0:T(8,128)(2,1)S(1)} %get-tuple-element.78), channel_id=1, source_target_pairs={{0,16},{4,20},{8,24},{12,28},{16,0},{20,4},{24,8},{28,12},{1,17},{... | collective-permute-start | bytes 41480 | tf_op jit(solution)/shard_map/ppermute | solution.py:117
  61.6 4.7 %collective-permute-start.19 = (bf16[9,768]{1,0:T(8,128)(2,1)S(1)}, bf16[9,768]{1,0:T(8,128)(2,1)S(1)}, u32[]{:S(2)}, u32[]{:S(2)}) collective-permute-start(bf16[9,768]{1,0:T(8,128)(2,1)S(1)} %get-tuple-element.79), channel_id=1, source_target_pairs={{0,24},{4,28},{8,16},{12,20},{16,8},{20,12},{24,0},{28,4},{1,25},{... | collective-permute-start | bytes 41480 | tf_op jit(solution)/shard_map/ppermute | solution.py:117
  66.5 1.3 %collective-permute-start.20 = (bf16[36,576]{1,0:T(8,128)(2,1)S(1)}, bf16[36,576]{1,0:T(8,128)(2,1)S(1)}, u32[]{:S(2)}, u32[]{:S(2)}) collective-permute-start(bf16[36,576]{1,0:T(8,128)(2,1)S(1)} %pad_maximum_fusion.3), channel_id=1, source_target_pairs={{0,4},{4,0},{8,12},{12,8},{16,20},{20,16},{24,28},{28,24},{1,5},{5... | collective-permute-start | bytes 124424 | tf_op jit(solution)/shard_map/ppermute | solution.py:117
